TPU v7x, 32 devices: a whole 2x2x4 slice. The times are simulated.
32 devices in a mesh: gx: 8 (over z, y), gy: 4 (over x, core).
Axes of the slice: x: 2, y: 2, z: 4, core: 2. Of those that a mesh axis runs over, the one named last changes fastest.
Arguments:
- state: float32 [2048, 1, 8, 2048], P('gx', None, None, 'gy'), may hold values from -1 to 1, as said below
- mobility: float32 [2048, 1, 2048], P('gx', None, 'gy'), may hold values from 0.22 to 4.5, as said below
Outputs:
- new_state: float32 [2048, 1, 8, 2048], P('gx', None, None, 'gy')
Inputs may be any that keep to these rules, and one draw needn't show every extreme that they name: `state`: each order parameter's value at a cell. Each cell's mobility.
All inputs are finite; a program needn't handle non-finite values.
Results may differ from a plain program's by a relative error of at most 0.0054.
Values sent between devices are 32-bit elements; how exact they have to be, the bound alone decides.
No kernel may reach another device: no remote copies, remote signals or barrier semaphores. Data moves between devices by JAX's collectives and lax.ppermute only.
A program may use at most 128 MiB of HBM per device.

v0:
```python
import math

import jax
import jax.numpy as jnp
from jax import lax
from jax.sharding import PartitionSpec as P

NX = 2048
NY = 2048


linear_coef = 1.0
cubic_coef = 1.0
cross_coef = 1.5
gradient_coef = 200.0
time_step = 200.0


def padded_2(cells, sides, width):
    for axis, dim in sides:
        count = lax.axis_size(axis)
        head = lax.slice_in_dim(cells, 0, width, axis=dim)
        tail = lax.slice_in_dim(cells, cells.shape[dim] - width, cells.shape[dim], axis=dim)
        cells = jnp.concatenate(
            [
                lax.ppermute(tail, axis, [(i, (i + 1) % count) for i in range(count)]),
                cells,
                lax.ppermute(head, axis, [((i + 1) % count, i) for i in range(count)]),
            ],
            axis=dim,
        )
    return cells


def hartley_table(positions, size):
    freqs = jnp.arange(size, dtype=jnp.int32)
    phase = positions[:, None] * freqs[None, :] % size
    angle = phase.astype(jnp.float32) * (2.0 * math.pi / size)
    return jnp.cos(angle) + jnp.sin(angle)


def symbol(freq_x, freq_y, size_x, size_y):
    sine_x = jnp.sin(freq_x * (math.pi / size_x))
    sine_y = jnp.sin(freq_y * (math.pi / size_y))
    return 1.0 + time_step * gradient_coef * (4.0 * sine_x * sine_x + 4.0 * sine_y * sine_y)


def laplace(field):
    padded = padded_2(field, (("gx", 0), ("gy", 3)), 1)
    inplane = (
        padded[:-2, :, :, 1:-1]
        + padded[2:, :, :, 1:-1]
        + padded[1:-1, :, :, :-2]
        + padded[1:-1, :, :, 2:]
        - 4.0 * field
    )
    lower = jnp.concatenate([field, field[:, :-1]], axis=1)
    upper = jnp.concatenate([field[:, 1:], field], axis=1)
    return inplane + lower + upper - 2.0 * field


def precondition(vector, x_table, y_table):
    rows_total = x_table.shape[0]
    highest = lax.Precision.HIGHEST
    piece = lax.all_to_all(vector, "gx", split_axis=3, concat_axis=0, tiled=True)
    flat = piece.reshape(rows_total, -1)
    product = jnp.dot(x_table, flat, precision=highest, preferred_element_type=jnp.float32)
    columns = product.reshape(piece.shape)
    pencil = lax.all_to_all(
        lax.all_to_all(columns, "gx", split_axis=0, concat_axis=3, tiled=True),
        "gy",
        split_axis=0,
        concat_axis=3,
        tiled=True,
    )
    local_rows = pencil.shape[0]
    cols_total = pencil.shape[3]
    spectrum = jnp.dot(
        pencil.reshape(-1, cols_total),
        y_table,
        precision=highest,
        preferred_element_type=jnp.float32,
    ).reshape(pencil.shape)
    offset = (
        lax.axis_index("gx") * (local_rows * lax.axis_size("gy"))
        + lax.axis_index("gy") * local_rows
    )
    freq_x = (offset + jnp.arange(local_rows, dtype=jnp.int32)).astype(jnp.float32)[
        :, None, None, None
    ]
    freq_y = jnp.arange(cols_total, dtype=jnp.float32)[None, None, None, :]
    scaled = spectrum / (
        symbol(freq_x, freq_y, rows_total, cols_total) * float(rows_total * cols_total)
    )
    back_rows = lax.dot_general(
        scaled.reshape(-1, cols_total),
        y_table,
        (((1,), (1,)), ((), ())),
        precision=highest,
        preferred_element_type=jnp.float32,
    )
    back_rows = back_rows.reshape(pencil.shape)
    returned = lax.all_to_all(
        lax.all_to_all(back_rows, "gy", split_axis=3, concat_axis=0, tiled=True),
        "gx",
        split_axis=3,
        concat_axis=0,
        tiled=True,
    )
    result = jnp.dot(
        x_table,
        returned.reshape(rows_total, -1),
        precision=highest,
        preferred_element_type=jnp.float32,
    )
    result = result.reshape(returned.shape)
    result = lax.all_to_all(result, "gx", split_axis=0, concat_axis=3, tiled=True)
    return result


def length(vector):
    return lax.psum(jnp.sum(vector * vector), ("gx", "gy"))


def project(basis, image):
    local = jnp.stack([jnp.sum(member * image) for member in basis])
    return lax.psum(local, ("gx", "gy"))


def least_squares(beta, top_left, below_first, top_right, middle_right, bottom_right):
    first_radius = jnp.sqrt(top_left * top_left + below_first * below_first)
    first_cosine = top_left / first_radius
    first_sine = below_first / first_radius
    upper_right = first_cosine * top_right + first_sine * middle_right
    lower_right = -first_sine * top_right + first_cosine * middle_right
    upper_target = first_cosine * beta
    lower_target = -first_sine * beta
    second_radius = jnp.sqrt(lower_right * lower_right + bottom_right * bottom_right)
    second_cosine = lower_right / second_radius
    second_coef = second_cosine * lower_target / second_radius
    first_coef = (upper_target - upper_right * second_coef) / first_radius
    return (first_coef, second_coef)


def body(state, mobility):
    x_table = hartley_table(jnp.arange(NX, dtype=jnp.int32), NX)
    y_positions = jnp.arange(NY, dtype=jnp.int32)
    y_table = hartley_table(y_positions, NY)
    squares = state * state
    total = jnp.sum(squares, axis=2, keepdims=True)
    reaction = -linear_coef + 3.0 * cubic_coef * squares + 2.0 * cross_coef * (total - squares)
    rate = time_step * mobility[:, :, None, :]
    force = rate * (
        -linear_coef * state
        + cubic_coef * squares * state
        + 2.0 * cross_coef * state * (total - squares)
        - gradient_coef * laplace(state)
    )
    start = -force
    beta = jnp.sqrt(length(start))
    basis = [start / beta]
    searches = []
    heights_all = []
    norms_all = []
    for iteration in range(2):
        search = precondition(basis[-1], x_table, y_table)
        coupled = jnp.sum(state * search, axis=2, keepdims=True)
        image = search + rate * (
            reaction * search
            + 4.0 * cross_coef * state * (coupled - state * search)
            - gradient_coef * laplace(search)
        )
        heights = project(basis, image)
        for position in range(len(basis)):
            image = image - heights[position] * basis[position]
        norm = jnp.sqrt(length(image))
        searches.append(search)
        heights_all.append(heights)
        norms_all.append(norm)
        if iteration == 0:
            basis.append(image / norm)
    first_coef, second_coef = least_squares(
        beta, heights_all[0][0], norms_all[0], heights_all[1][0], heights_all[1][1], norms_all[1]
    )
    update = first_coef * searches[0] + second_coef * searches[1]
    return state + update


def solution(mesh):
    return jax.shard_map(
        body,
        mesh=mesh,
        in_specs=(P("gx", None, None, "gy"), P("gx", None, "gy")),
        out_specs=P("gx", None, None, "gy"),
        check_vma=False,
    )
```

profile of v0, /device:TPU:0, one launch (start us, length us, event | category | flops | bytes accessed | tf_op | source)
XLA Modules:
  0.0 2154.9 jit_solution(4567546493117916038)
XLA Ops:
  22.6 15.1 multiply_reduce_fusion.5
  37.8 38.1 %psum.35 = f32[]{:T(128)} all-reduce(f32[]{:T(128)} %get-tuple-element.10), channel_id=1, replica_groups=mesh['gx'=8,'gy'=4] {'gx','gy'}, use_global_device_ids=true, to_apply=%region_2.3 | all-reduce | flops 1 | bytes 8 | tf_op jit(solution)/shard_map/psum | solution.py:122
  89.8 67.1 %fusion.137 = f32[2048,2048,1]{1,0,2:T(8,128)} fusion(), kind=kLoop, calls=%fused_computation.21.clone.clone.clone.1 | loop fusion | flops 62914560 | bytes 16777216 | tf_op jit(solution)/shard_map/dot_general | solution.py:67
  156.9 25.3 %all-to-all-done = f32[256,1,8,512]{0,2,1,3:T(8,128)} async-done(((f32[256,1,8,512]{0,2,1,3:T(8,128)}), f32[256,1,8,512]{0,2,1,3:T(8,128)}, u32[]{:S(2)}, u32[]{:S(2)}) %all-to-all-start) | async-done | bytes 4194336 | tf_op jit(solution)/shard_map/all_to_all | solution.py:65
  191.5 28.7 %fusion.50 = f32[2048,1,8,64]{0,3,2,1:T(8,128)} fusion(f32[8,64,2048]{2,1,0:T(8,128)S(1)} %bitcast.215, f32[2048,2048,1]{1,0,2:T(8,128)S(1)} %copy-done.9), kind=kOutput, calls=%fused_computation.93 | convolution fusion | flops 25769803776 | bytes 25165824 | tf_op jit(solution)/shard_map/dot_general | solution.py:67
  237.0 97.5 %all_to_all.198 = f32[8,1,131072]{2,1,0:T(1,128)} all-to-all(f32[8,1,131072]{2,1,0:T(1,128)} %reshape.252), channel_id=1, replica_groups=mesh['gx'=8,'gy'=4] {'gx'}, dimensions={0} | all-to-all | bytes 8388608 | tf_op jit(solution)/shard_map/all_to_all | solution.py:70
  379.8 67.1 %fusion.135 = f32[2048,2048,1]{1,0,2:T(8,128)} fusion(), kind=kLoop, calls=%fused_computation.19.clone | loop fusion | flops 62914560 | bytes 16777216 | tf_op jit(solution)/shard_map/dot_general | solution.py:78
  461.1 31.8 %fusion.15 = f32[64,8,2048]{2,1,0:T(8,128)S(1)} fusion(f32[64,8,2048]{2,1,0:T(8,128)} %dot_general.51, f32[2048,2048,1]{1,0,2:T(8,128)} %fusion.135), kind=kOutput, calls=%fused_computation.18 | convolution fusion | flops 25769803776 | bytes 25165824 | tf_op jit(solution)/shard_map/dot_general | solution.py:78
  493.7 94.6 %fusion.53 = f32[64,1,8,2048]{3,2,0,1:T(8,128)} fusion(f32[64,8,2048]{2,1,0:T(8,128)S(1)} %fusion.139), kind=kOutput, calls=%fused_computation.94 | convolution fusion | flops 25832718336 | bytes 8388608 | tf_op jit(solution)/shard_map/dot_general | solution.py:95
  604.5 53.9 %all_to_all.199 = f32[4,1,262144]{2,1,0:T(1,128)} all-to-all(f32[4,1,262144]{2,1,0:T(1,128)} %reshape.254), channel_id=1, replica_groups=mesh['gx'=8,'gy'=4] {'gy'}, dimensions={0} | all-to-all | bytes 8388608 | tf_op jit(solution)/shard_map/all_to_all | solution.py:104
  658.3 15.2 reduce.4
  706.5 67.1 %fusion.141 = f32[2048,2048,1]{1,0,2:T(8,128)} fusion(), kind=kLoop, calls=%fused_computation.15.clone.clone.clone | loop fusion | flops 62914560 | bytes 16777216 | tf_op jit(solution)/shard_map/dot_general | solution.py:110
  773.7 26.0 %all-to-all-done.4 = f32[256,1,8,512]{0,2,1,3:T(8,128)} async-done(((f32[256,1,8,512]{0,2,1,3:T(8,128)}), f32[256,1,8,512]{0,2,1,3:T(8,128)}, u32[]{:S(2)}, u32[]{:S(2)}) %all-to-all-start.4) | async-done | bytes 4194336 | tf_op jit(solution)/shard_map/all_to_all | solution.py:103
  808.9 28.7 %fusion.58 = f32[2048,1,8,64]{0,3,2,1:T(8,128)} fusion(f32[8,64,2048]{2,1,0:T(8,128)S(1)} %bitcast.216, f32[2048,2048,1]{1,0,2:T(8,128)S(1)} %copy-done.10), kind=kOutput, calls=%fused_computation.95 | convolution fusion | flops 25769803776 | bytes 25165824 | tf_op jit(solution)/shard_map/dot_general | solution.py:110
  854.4 97.5 %all_to_all.200 = f32[8,1,131072]{2,1,0:T(1,128)} all-to-all(f32[8,1,131072]{2,1,0:T(1,128)} %reshape.256), channel_id=1, replica_groups=mesh['gx'=8,'gy'=4] {'gx'}, dimensions={0} | all-to-all | bytes 8388608 | tf_op jit(solution)/shard_map/all_to_all | solution.py:117
  1017.0 37.2 %psum.36 = f32[]{:T(128)} all-reduce(f32[]{:T(128)} %get-tuple-element.8), channel_id=1, replica_groups=mesh['gx'=8,'gy'=4] {'gx','gy'}, use_global_device_ids=true, to_apply=%region_5.6 | all-reduce | flops 1 | bytes 8 | tf_op jit(solution)/shard_map/psum | solution.py:127
  1060.0 41.8 %psum.37 = f32[]{:T(128)} all-reduce(f32[]{:T(128)} %multiply_reduce_fusion.3), channel_id=1, replica_groups=mesh['gx'=8,'gy'=4] {'gx','gy'}, use_global_device_ids=true, to_apply=%region_7.8 | all-reduce | flops 1 | bytes 8 | tf_op jit(solution)/shard_map/psum | solution.py:122
  1118.9 67.1 %fusion.143 = f32[2048,2048,1]{1,0,2:T(8,128)} fusion(), kind=kLoop, calls=%fused_computation.13.clone.clone.clone | loop fusion | flops 62914560 | bytes 16777216 | tf_op jit(solution)/shard_map/dot_general | solution.py:67
  1186.0 25.5 %all-to-all-done.6 = f32[256,1,8,512]{0,2,1,3:T(8,128)} async-done(((f32[256,1,8,512]{0,2,1,3:T(8,128)}), f32[256,1,8,512]{0,2,1,3:T(8,128)}, u32[]{:S(2)}, u32[]{:S(2)}) %all-to-all-start.6) | async-done | bytes 4194336 | tf_op jit(solution)/shard_map/all_to_all | solution.py:65
  1220.8 28.8 %fusion.61 = f32[2048,1,8,64]{0,3,2,1:T(8,128)} fusion(f32[8,64,2048]{2,1,0:T(8,128)S(1)} %bitcast.217, f32[2048,2048,1]{1,0,2:T(8,128)S(1)} %copy-done.11), kind=kOutput, calls=%fused_computation.96 | convolution fusion | flops 25769803776 | bytes 25165824 | tf_op jit(solution)/shard_map/dot_general | solution.py:67
  1266.3 97.5 %all_to_all.201 = f32[8,1,131072]{2,1,0:T(1,128)} all-to-all(f32[8,1,131072]{2,1,0:T(1,128)} %reshape.258), channel_id=1, replica_groups=mesh['gx'=8,'gy'=4] {'gx'}, dimensions={0} | all-to-all | bytes 8388608 | tf_op jit(solution)/shard_map/all_to_all | solution.py:70
  1408.6 67.1 %fusion.133 = f32[2048,2048,1]{1,0,2:T(8,128)} fusion(), kind=kLoop, calls=%fused_computation.11.clone.1 | loop fusion | flops 62914560 | bytes 16777216 | tf_op jit(solution)/shard_map/dot_general | solution.py:78
  1490.0 31.5 %fusion.7 = f32[64,8,2048]{2,1,0:T(8,128)S(1)} fusion(f32[64,8,2048]{2,1,0:T(8,128)} %dot_general.61, f32[2048,2048,1]{1,0,2:T(8,128)} %fusion.133), kind=kOutput, calls=%fused_computation.10 | convolution fusion | flops 25769803776 | bytes 25165824 | tf_op jit(solution)/shard_map/dot_general | solution.py:78
  1522.5 94.8 %fusion.64 = f32[64,1,8,2048]{3,2,0,1:T(8,128)} fusion(f32[64,8,2048]{2,1,0:T(8,128)S(1)} %fusion.145), kind=kOutput, calls=%fused_computation.97 | convolution fusion | flops 25832718336 | bytes 8388608 | tf_op jit(solution)/shard_map/dot_general | solution.py:95
  1633.4 53.9 %all_to_all.202 = f32[4,1,262144]{2,1,0:T(1,128)} all-to-all(f32[4,1,262144]{2,1,0:T(1,128)} %reshape.260), channel_id=1, replica_groups=mesh['gx'=8,'gy'=4] {'gy'}, dimensions={0} | all-to-all | bytes 8388608 | tf_op jit(solution)/shard_map/all_to_all | solution.py:104
  1687.3 15.2 reduce.7
  1735.2 67.1 %fusion.147 = f32[2048,2048,1]{1,0,2:T(8,128)} fusion(), kind=kLoop, calls=%fused_computation.7.clone.clone.clone | loop fusion | flops 62914560 | bytes 16777216 | tf_op jit(solution)/shard_map/dot_general | solution.py:110
  1802.4 26.0 %all-to-all-done.10 = f32[256,1,8,512]{0,2,1,3:T(8,128)} async-done(((f32[256,1,8,512]{0,2,1,3:T(8,128)}), f32[256,1,8,512]{0,2,1,3:T(8,128)}, u32[]{:S(2)}, u32[]{:S(2)}) %all-to-all-start.10) | async-done | bytes 4194336 | tf_op jit(solution)/shard_map/all_to_all | solution.py:103
  1837.6 28.8 %fusion.69 = f32[2048,1,8,64]{0,3,2,1:T(8,128)} fusion(f32[8,64,2048]{2,1,0:T(8,128)S(1)} %bitcast.218, f32[2048,2048,1]{1,0,2:T(8,128)S(1)} %copy-done.12), kind=kOutput, calls=%fused_computation.98 | convolution fusion | flops 25769803776 | bytes 25165824 | tf_op jit(solution)/shard_map/dot_general | solution.py:110
  1883.2 97.6 %all_to_all.203 = f32[8,1,131072]{2,1,0:T(1,128)} all-to-all(f32[8,1,131072]{2,1,0:T(1,128)} %reshape.262), channel_id=1, replica_groups=mesh['gx'=8,'gy'=4] {'gx'}, dimensions={0} | all-to-all | bytes 8388608 | tf_op jit(solution)/shard_map/all_to_all | solution.py:117
  2051.4 37.0 %psum.38 = f32[2]{0:T(128)S(1)} all-reduce(f32[2]{0:T(128)S(1)} %pad_maximum_fusion.33), channel_id=1, replica_groups=mesh['gx'=8,'gy'=4] {'gx','gy'}, use_global_device_ids=true, to_apply=%region_11.12 | all-reduce | flops 2 | bytes 16 | tf_op jit(solution)/shard_map/psum | solution.py:127
  2099.0 41.7 %psum.39 = f32[]{:T(128)} all-reduce(f32[]{:T(128)} %multiply_reduce_fusion), channel_id=1, replica_groups=mesh['gx'=8,'gy'=4] {'gx','gy'}, use_global_device_ids=true, to_apply=%region_13.14 | all-reduce | flops 1 | bytes 8 | tf_op jit(solution)/shard_map/psum | solution.py:122
  (174 shorter events, 534.8 us)
Async XLA Ops:
  0.7 13.8 collective-permute-start
  3.7 11.5 collective-permute-start.1
  14.5 8.1 copy-start.13
  18.3 4.3 collective-permute-start.2
  18.4 4.3 collective-permute-start.3
  22.6 15.2 copy-start.16
  83.6 98.6 %all-to-all-start = ((f32[256,1,8,512]{0,2,1,3:T(8,128)}), f32[256,1,8,512]{0,2,1,3:T(8,128)}, u32[]{:S(2)}, u32[]{:S(2)}) async-start(f32[256,1,8,512]{0,2,1,3:T(8,128)} %copy.209), calls=%async_computation | async-start | bytes 8388608 | tf_op jit(solution)/shard_map/all_to_all | solution.py:65
  185.7 5.8 copy-start.9
  374.4 72.5 %all-to-all-start.2 = ((f32[256,1,8,512]{3,2,1,0:T(8,128)}), f32[256,1,8,512]{3,2,1,0:T(8,128)}, u32[]{:S(2)}, u32[]{:S(2)}) async-start(f32[256,1,8,512]{3,2,1,0:T(8,128)} %copy.215), calls=%async_computation.2 | async-start | bytes 8388608 | tf_op jit(solution)/shard_map/all_to_all | solution.py:69
  379.8 113.0 %copy-start.19 = (f32[64,2048]{1,0:T(8,128)}, f32[64,2048]{1,0:T(8,128)S(1)}, u32[]{:S(2)}) copy-start(f32[64,2048]{1,0:T(8,128)S(1)} %add_multiply_fusion) | copy-start | bytes 1572868
  701.5 98.1 %all-to-all-start.4 = ((f32[256,1,8,512]{0,2,1,3:T(8,128)}), f32[256,1,8,512]{0,2,1,3:T(8,128)}, u32[]{:S(2)}, u32[]{:S(2)}) async-start(f32[256,1,8,512]{0,2,1,3:T(8,128)} %copy.220), calls=%async_computation.4 | async-start | bytes 8388608 | tf_op jit(solution)/shard_map/all_to_all | solution.py:103
  803.2 5.8 copy-start.10
  986.9 10.9 collective-permute-start.4
  989.3 9.3 collective-permute-start.5
  1001.7 3.7 collective-permute-start.6
  1001.8 4.3 copy-start.8
  1001.8 4.3 copy-start.14
  1001.8 4.5 copy-start.17
  1001.8 3.6 collective-permute-start.7
  1113.9 97.6 %all-to-all-start.6 = ((f32[256,1,8,512]{0,2,1,3:T(8,128)}), f32[256,1,8,512]{0,2,1,3:T(8,128)}, u32[]{:S(2)}, u32[]{:S(2)}) async-start(f32[256,1,8,512]{0,2,1,3:T(8,128)} %copy.234), calls=%async_computation.6 | async-start | bytes 8388608 | tf_op jit(solution)/shard_map/all_to_all | solution.py:65
  1215.0 5.8 copy-start.11
  1403.3 72.5 %all-to-all-start.8 = ((f32[256,1,8,512]{3,2,1,0:T(8,128)}), f32[256,1,8,512]{3,2,1,0:T(8,128)}, u32[]{:S(2)}, u32[]{:S(2)}) async-start(f32[256,1,8,512]{3,2,1,0:T(8,128)} %copy.240), calls=%async_computation.8 | async-start | bytes 8388608 | tf_op jit(solution)/shard_map/all_to_all | solution.py:69
  1490.0 31.5 %copy-start.20 = (f32[64,2048]{1,0:T(8,128)S(1)}, f32[64,2048]{1,0:T(8,128)}, u32[]{:S(2)}) copy-start(f32[64,2048]{1,0:T(8,128)} %copy-done.19) | copy-start | bytes 1572868
  1730.5 97.8 %all-to-all-start.10 = ((f32[256,1,8,512]{0,2,1,3:T(8,128)}), f32[256,1,8,512]{0,2,1,3:T(8,128)}, u32[]{:S(2)}, u32[]{:S(2)}) async-start(f32[256,1,8,512]{0,2,1,3:T(8,128)} %copy.245), calls=%async_computation.10 | async-start | bytes 8388608 | tf_op jit(solution)/shard_map/all_to_all | solution.py:103
  1831.9 5.8 copy-start.12
  2015.7 12.9 collective-permute-start.8
  2018.0 11.2 collective-permute-start.9
  2023.2 12.9 copy-start.18
  2032.5 3.6 collective-permute-start.10
  2032.6 4.8 copy-start.7
  2032.6 4.8 copy-start.15
  2032.6 3.5 collective-permute-start.11
  (8 other events, 25.3 us)
where the time goes:
time: 2170 us; the launch traced here: 2150 us
  blocking collectives  694 us (32%)
  other arithmetic  568 us (26%)
  matrix products  368 us (17%)
  local copies, waits for them, and re-layouts  363 us (17%)
  waiting for transfers between devices  103 us (5%)
  starting transfers between devices  52.2 us (2%)
    all_to_all x2, blocking collectives, precondition(): lax.all_to_all(result, 'gx', split_axis=0, concat_axis=3, tiled=True)  195 us
    all_to_all x2, blocking collectives, precondition(): lax.all_to_all(columns, 'gx', split_axis=0, concat_axis=3, tiled=True)  195 us
    dot_general x2, matrix products, precondition(): lax.dot_general(scaled.reshape(-1, cols_total), y_table, (((1,), (1,)), (...  189 us
    dot_general x2, other arithmetic, precondition(): jnp.dot(x_table, flat, precision=highest, preferred_element_type=jnp.floa...  134 us
    dot_general x2, other arithmetic, precondition(): jnp.dot(x_table, returned.reshape(rows_total, -1), precision=highest, pre...  134 us
    dot_general x2, other arithmetic, precondition(): jnp.dot(pencil.reshape(-1, cols_total), y_table, precision=highest, prefe...  134 us
    unnamed x61, local copies, waits for them, and re-layouts  134 us
    psum x3, blocking collectives, length(): return lax.psum(jnp.sum(vector * vector), ('gx', 'gy'))  122 us
  transfers between devices with their start and end apart: 18, of which 4 were waited for; matrix products, arithmetic and copies ran while one was open for 20% of the time, Pallas kernels for 0%

commit v1 on v0

v1 whole, which is shorter than its diff:
```python
import functools
import math

import jax
import jax.numpy as jnp
import numpy as np
from jax import lax
from jax.experimental import pallas as pl
from jax.experimental.pallas import tpu as pltpu
from jax.sharding import PartitionSpec as P

linear_coef = 1.0
cubic_coef = 1.0
cross_coef = 1.5
gradient_coef = 200.0
time_step = 200.0
stiffness = time_step * gradient_coef

F32 = jnp.float32
BF16 = jnp.bfloat16
VMEM_LIMIT = 56 * 1024 * 1024


def cosine_table(size):
    modes = np.arange(size)[:, None]
    cells = np.arange(size)[None, :]
    table = np.sqrt(2.0 / size) * np.cos(np.pi * modes * (cells + 0.5) / size)
    table[0] = np.sqrt(1.0 / size)
    values = 4.0 * np.sin(np.pi * np.arange(size) / (2 * size)) ** 2
    order = np.concatenate([np.arange(0, size, 2), np.arange(1, size, 2)])
    return table[order], values[order]


def split_const(table):
    high = table.astype(np.float32).astype(jnp.bfloat16)
    low = (table - high.astype(np.float64)).astype(np.float32).astype(jnp.bfloat16)
    return high, low


def right_const(table):
    high, low = split_const(table)
    return np.concatenate([high, low, high], axis=0)


def left_const(table):
    high, low = split_const(table)
    return np.concatenate([high, low, high], axis=1)


def make_tables(lx, ly, gx, gy):
    cos_x, value_x = cosine_table(lx)
    cos_y, value_y = cosine_table(ly)
    edge_x, edge_y = cos_x[:, 0], cos_y[:, 0]
    inverse = 1.0 / (1.0 + stiffness * (value_x[:, None] + value_y[None, :]))
    cross = edge_x[:, None] * edge_y[None, :] * inverse
    sign_x = np.where(np.arange(lx) < lx // 2, 1.0, -1.0)
    sign_y = np.where(np.arange(ly) < ly // 2, 1.0, -1.0)
    own = (edge_x[:, None] ** 2 * inverse).sum(0)
    other = (sign_x[:, None] * edge_x[:, None] ** 2 * inverse).sum(0)
    wave = np.arange(gx)
    eigen = 1.0 / stiffness + 2.0 * own[None] - 2.0 * other[None] * np.cos(2 * np.pi * wave / gx)[:, None]
    gap_x = np.stack(
        [(np.cos(2 * np.pi * wave * d / gx)[:, None] / eigen).mean(0) for d in range(gx // 2 + 1)]
    )
    total = lx * gx
    half = gx // 2 + 1
    rows = -(-half * gy // 8) * 8
    freq = gx * np.arange(lx)[None, :] + np.arange(half)[:, None]
    symbol = 1.0 + stiffness * (4.0 * np.sin(np.pi * freq / total) ** 2)[:, :, None] + stiffness * value_y
    own = (edge_y**2 / symbol).sum(-1)
    other = (sign_y * edge_y**2 / symbol).sum(-1)
    wave = np.arange(gy)
    eigen = 1.0 / stiffness + 2.0 * own[None] - 2.0 * other[None] * np.cos(2 * np.pi * wave / gy)[:, None, None]
    gap_y = np.zeros((gy // 2 + 1, 2 * rows, lx))
    for d in range(gy // 2 + 1):
        coef = (np.cos(2 * np.pi * wave * d / gy)[:, None, None] / eigen).mean(0)
        coef = np.repeat(coef, gy, axis=0)
        gap_y[d, : half * gy] = coef
        gap_y[d, rows : rows + half * gy] = coef
    cells = np.arange(lx)
    angle = 2 * np.pi * np.outer(cells, cells) / lx
    fourier = np.concatenate([np.cos(angle), np.sin(angle)], axis=1)
    twist = np.zeros((2, rows, lx))
    gather = np.zeros((2 * rows, gx * gy))
    scatter = np.zeros((gx * gy, 2 * rows))
    for q in range(half):
        theta = 2 * np.pi * q * cells / total
        weight = (1.0 if q in (0, gx // 2) else 2.0) / total
        for j in range(gy):
            twist[0, q * gy + j] = np.cos(theta)
            twist[1, q * gy + j] = np.sin(theta)
            for i in range(gx):
                phase = 2 * np.pi * q * i / gx
                gather[q * gy + j, i * gy + j] = np.cos(phase)
                gather[rows + q * gy + j, i * gy + j] = -np.sin(phase)
                scatter[i * gy + j, q * gy + j] = weight * np.cos(phase)
                scatter[i * gy + j, rows + q * gy + j] = -weight * np.sin(phase)
    single = lambda a: np.ascontiguousarray(a, dtype=np.float32)
    zero_x, zero_y = np.zeros(lx // 2), np.zeros(ly // 2)
    ends_x = np.zeros((8, lx))
    ends_x[0], ends_x[1] = (
        np.concatenate([edge_x[: lx // 2], zero_x]),
        np.concatenate([zero_x, edge_x[lx // 2 :]]),
    )
    ends_y = np.zeros((8, ly))
    ends_y[2], ends_y[3] = (
        np.concatenate([edge_y[: ly // 2], zero_y]),
        np.concatenate([zero_y, edge_y[ly // 2 :]]),
    )
    main = dict(
        fwd_y=right_const(cos_y.T),
        fwd_x=left_const(cos_x),
        inv_y=right_const(cos_y),
        inv_x=left_const(cos_x.T),
        inverse=single(inverse),
        edge_x=single(edge_x[:, None]),
        edge_y=single(edge_y[None, :]),
        ends_x=single(ends_x),
        ends_y=single(ends_y),
    )
    face = dict(
        cross=single(cross),
        cross_t=single(cross.T),
        cos_x=single(cos_x),
        cos_xt=single(cos_x.T),
        gap_x=single(gap_x),
        gap_y=single(gap_y),
        fourier=single(fourier),
        twist=single(twist),
        gather=single(gather),
        scatter=single(scatter),
    )
    return main, face


def halves(x):
    high = x.astype(BF16)
    low = (x - high.astype(F32)).astype(BF16)
    return high, low


def times_right(x, const):
    high, low = halves(x)
    return jnp.dot(jnp.concatenate([high, high, low], axis=1), const[...], preferred_element_type=F32)


def times_left(const, x):
    high, low = halves(x)
    return jnp.dot(const[...], jnp.concatenate([high, high, low], axis=0), preferred_element_type=F32)


def thirds(x):
    high = x.astype(BF16).astype(F32)
    rest = x - high
    mid = rest.astype(BF16).astype(F32)
    return high, mid, rest - mid


def outer_sum(a, b):
    ah, am, al = thirds(a)
    bh, bm, bl = thirds(b)
    left = jnp.concatenate([ah, ah, am, am, ah, al], axis=0).astype(BF16)
    right = jnp.concatenate([bh, bm, bh, bm, bl, bh], axis=0).astype(BF16)
    return lax.dot_general(left, right, (((0,), (0,)), ((), ())), preferred_element_type=F32)


def transform_out(field, k, spec, pay, tabs, dest):
    lx, ly = field.shape[1:]
    hat = times_left(tabs["fwd_x"], times_right(field[k], tabs["fwd_y"]))
    spectrum = hat * tabs["inverse"][...]
    spec[k] = spectrum
    weighted = spectrum * tabs["edge_x"][...]
    top = [
        jnp.sum(weighted[: lx // 2], axis=0, keepdims=True),
        jnp.sum(weighted[lx // 2 :], axis=0, keepdims=True),
    ]
    weighted = spectrum * tabs["edge_y"][...]
    cols = [weighted[:, i * 128 : (i + 1) * 128] for i in range(ly // 128)]
    half = len(cols) // 2
    folded = jnp.concatenate([sum(cols[1:half], cols[0]), sum(cols[half + 1 :], cols[half])], axis=0)
    high, low = halves(folded)
    ones = jnp.ones((8, 256), BF16)
    side = lax.dot_general(
        ones, jnp.concatenate([high, low], axis=1), (((1,), (1,)), ((), ())), preferred_element_type=F32
    )[:1]
    line = jnp.concatenate([*top, side], axis=1)
    for d in dest(k):
        for j in range(line.shape[1] // 128):
            pay[d, j : j + 1, :] = line[:, j * 128 : (j + 1) * 128]


def transform_back(spec, k, corr, field, tabs):
    lx, ly = field.shape[1:]
    nx, ny = lx // 128, ly // 128
    piece = lambda start, count: jnp.concatenate(
        [corr[k, start + j : start + j + 1, :] for j in range(count)], axis=1
    )
    row = lax.broadcasted_iota(jnp.int32, (8, 1), 0)
    a = (
        tabs["ends_x"][...]
        + jnp.where(row == 2, piece(2 * ny, nx), 0.0)
        + jnp.where(row == 3, piece(2 * ny + nx, nx), 0.0)
    )
    b = (
        tabs["ends_y"][...]
        + jnp.where(row == 0, piece(0, ny), 0.0)
        + jnp.where(row == 1, piece(ny, ny), 0.0)
    )
    spectrum = spec[k] + tabs["inverse"][...] * outer_sum(a, b)
    return times_left(tabs["inv_x"], times_right(spectrum, tabs["inv_y"]))


def lane_sum(x):
    return jnp.sum(x, axis=0, keepdims=True)


def store_sums(pay, start, rows):
    for j, row in enumerate(rows):
        for d in range(pay.shape[0]):
            pay[d, start + j : start + j + 1, :] = row


MAIN = ("fwd_y", "fwd_x", "inv_y", "inv_x", "inverse", "edge_x", "edge_y", "ends_x", "ends_y")
FACE = (
    "cross",
    "cross_t",
    "cos_x",
    "cos_xt",
    "gap_x",
    "gap_y",
    "fourier",
    "twist",
    "gather",
    "scatter",
)


def destinations(k, kinds, gx, gy):
    return [k * gy + p + kinds * gy * copy for copy in range(gx // kinds) for p in range(gy)]


def start_kernel(gx, gy, nrow, *refs):
    state, mob_hbm, edge_lo, edge_hi, side = refs[:5]
    tabs = dict(zip(("fwd_y", "fwd_x", "inverse", "edge_x", "edge_y"), refs[5:10]))
    r0_out, spec_out, pay = refs[10:13]
    st, mob, field, spec, acc, sem, out_sem = refs[13:]
    kinds, lx, ly = field.shape
    copies = [
        pltpu.make_async_copy(state.at[:, 0, k, :], st.at[k, pl.ds(8, lx), :], sem.at[k]) for k in range(kinds)
    ]
    for copy in copies:
        copy.start()
    mob_copy = pltpu.make_async_copy(mob_hbm.at[:, 0, :], mob, sem.at[kinds])
    mob_copy.start()
    for k in range(kinds):
        st[k, 7:8, :] = edge_lo[0, 0, k : k + 1, :]
        st[k, lx + 8 : lx + 9, :] = edge_hi[0, 0, k : k + 1, :]
    acc[...] = jnp.zeros_like(acc)
    mob_copy.wait()
    for copy in copies:
        copy.wait()
    lane = lax.broadcasted_iota(jnp.int32, (8, ly), 1)

    @pl.loop(0, lx // 8)
    def _(i):
        row = pl.multiple_of(i * 8, 8)
        rate = time_step * mob[pl.ds(row, 8), :]
        tall = [st[k, pl.ds(row, 24), :] for k in range(kinds)]
        mids = [block[8:16] for block in tall]
        total = sum(m * m for m in mids)
        base = -linear_coef + 2.0 * cross_coef * total
        norm = jnp.zeros((8, ly), F32)
        for k in range(kinds):
            mid = mids[k]
            around = tall[k][7:15] + tall[k][9:17]
            beside = side[k, pl.ds(row, 8), :]
            left = jnp.where(lane == 0, beside[:, 0:1], pltpu.roll(mid, 1, 1))
            right = jnp.where(lane == ly - 1, beside[:, 1:2], pltpu.roll(mid, ly - 1, 1))
            lap = around + left + right - 4.0 * mid
            react = mid * (base + (cubic_coef - 2.0 * cross_coef) * (mid * mid))
            value = rate * (gradient_coef * lap - react)
            field[k, pl.ds(row, 8), :] = value
            norm = norm + value * value
        acc[...] += sum(norm[:, j * 128 : (j + 1) * 128] for j in range(ly // 128))

    out = pltpu.make_async_copy(field, r0_out, out_sem.at[0])
    out.start()

    @pl.loop(0, kinds)
    def _(k):
        transform_out(field, k, spec, pay, tabs, lambda k: destinations(k, kinds, gx, gy))

    spec_copy = pltpu.make_async_copy(spec, spec_out, out_sem.at[1])
    spec_copy.start()
    store_sums(pay, nrow, [lane_sum(acc[...])])
    out.wait()
    spec_copy.wait()


def load_all(sources, kinds, sem):
    copies = [pltpu.make_async_copy(s, d, sem.at[j]) for j, (s, d) in enumerate(sources)]
    for copy in copies:
        copy.start()
    return copies


def middle_kernel(gx, gy, nrow, *refs):
    corr, state, mob_hbm, spec_in, r0_in = refs[:5]
    tabs = dict(zip(MAIN, refs[5:14]))
    z_out, q_out, spec_out, pay = refs[14:18]
    st, mob, spec, field, r0, acc, sem, out_sem = refs[18:]
    kinds, lx, ly = field.shape
    sources = [(spec_in, spec), (r0_in, r0), (mob_hbm.at[:, 0, :], mob)]
    sources += [(state.at[:, 0, k, :], st.at[k]) for k in range(kinds)]
    copies = load_all(sources, kinds, sem)
    acc[...] = jnp.zeros_like(acc)
    copies[0].wait()

    @pl.loop(0, kinds)
    def _(k):
        field[k] = transform_back(spec, k, corr, field, tabs)

    z_copy = pltpu.make_async_copy(field, z_out, out_sem.at[0])
    z_copy.start()
    for copy in copies[1:]:
        copy.wait()

    @pl.loop(0, lx // 8)
    def _(i):
        row = pl.multiple_of(i * 8, 8)
        for j in range(ly // 128):
            at = (pl.ds(row, 8), slice(j * 128, (j + 1) * 128))
            move = mob[at]
            rate = time_step * move
            s = [st[(k, *at)] for k in range(kinds)]
            z = [field[(k, *at)] for k in range(kinds)]
            squares = [v * v for v in s]
            total = sum(squares)
            coupled = sum(a * b for a, b in zip(s, z))
            base = 1.0 - move + rate * (-linear_coef + 2.0 * cross_coef * total)
            square_coef = (3.0 * cubic_coef - 6.0 * cross_coef) * rate
            pull = (4.0 * cross_coef) * rate * coupled
            part = jnp.zeros((8, 128), F32)
            for k in range(kinds):
                old = r0[(k, *at)]
                image = z[k] * (base + square_coef * squares[k]) + pull * s[k] + move * old
                r0[(k, *at)] = image
                part = part + old * image
            acc[...] += part

    q_copy = pltpu.make_async_copy(r0, q_out, out_sem.at[1])
    q_copy.start()

    @pl.loop(0, kinds)
    def _(k):
        transform_out(r0, k, spec, pay, tabs, lambda k: destinations(k, kinds, gx, gy))

    spec_copy = pltpu.make_async_copy(spec, spec_out, out_sem.at[2])
    spec_copy.start()
    store_sums(pay, nrow, [lane_sum(acc[...])])
    z_copy.wait()
    q_copy.wait()
    spec_copy.wait()


def last_kernel(gx, gy, nrow, *refs):
    corr, beta_sq, state, mob_hbm, spec_in, r0_in, q_in, z_in = refs[:8]
    tabs = dict(zip(("inv_y", "inv_x", "inverse", "ends_x", "ends_y"), refs[8:13]))
    z_out, sums = refs[13:15]
    st, mob, spec, field, r0, q1, acc, sem, out_sem = refs[15:]
    kinds, lx, ly = field.shape
    sources = [(spec_in, spec), (z_in, field), (r0_in, r0), (q_in, q1), (mob_hbm.at[:, 0, :], mob)]
    sources += [(state.at[:, 0, k, :], st.at[k]) for k in range(kinds)]
    copies = load_all(sources, kinds, sem)
    acc[...] = jnp.zeros_like(acc)
    height = corr[0, nrow : nrow + 1, :] / beta_sq[0, nrow : nrow + 1, :]
    copies[0].wait()
    copies[1].wait()

    @pl.loop(0, kinds)
    def _(k):
        field[k] = transform_back(spec, k, corr, field, tabs) - height[:, :1] * field[k]

    z_copy = pltpu.make_async_copy(field, z_out, out_sem.at[0])
    z_copy.start()
    for copy in copies[2:]:
        copy.wait()

    @pl.loop(0, lx // 8)
    def _(i):
        row = pl.multiple_of(i * 8, 8)
        for j in range(ly // 128):
            at = (pl.ds(row, 8), slice(j * 128, (j + 1) * 128))
            move = mob[at]
            rate = time_step * move
            s = [st[(k, *at)] for k in range(kinds)]
            z = [field[(k, *at)] for k in range(kinds)]
            squares = [v * v for v in s]
            total = sum(squares)
            coupled = sum(a * b for a, b in zip(s, z))
            base = 1.0 - move + rate * (-linear_coef + 2.0 * cross_coef * total)
            square_coef = (3.0 * cubic_coef - 6.0 * cross_coef) * rate
            pull = (4.0 * cross_coef) * rate * coupled
            parts = [jnp.zeros((8, 128), F32)] * 4
            for k in range(kinds):
                old = r0[(k, *at)]
                basis = q1[(k, *at)] - height * old
                image = z[k] * (base + square_coef * squares[k]) + pull * s[k] + move * basis
                pairs = ((basis, basis), (basis, image), (old, image), (image, image))
                parts = [p + a * b for p, (a, b) in zip(parts, pairs)]
            for n in range(4):
                acc[n] += parts[n]

    rows = [lane_sum(acc[n]) for n in range(4)]
    for d in range(sums.shape[0]):
        for n in range(4):
            sums[d, n : n + 1, :] = rows[n]
    z_copy.wait()


def face_kernel(gx, gy, lx, ly, nrow, place, pay, *refs):
    tabs = dict(zip(FACE, refs))
    out = refs[len(FACE)]
    nx, ny = lx // 128, ly // 128
    hx, hy = lx // 2, ly // 2
    blocks = gx * gy
    dot = functools.partial(jnp.dot, precision=lax.Precision.HIGHEST, preferred_element_type=F32)
    piece = lambda start, count: jnp.concatenate([pay[:, start + j, :] for j in range(count)], axis=1)
    t_even, t_odd = piece(0, ny), piece(ny, ny)
    s_even, s_odd = piece(2 * ny, nx), piece(2 * ny + nx, nx)

    def turn(a, shift):
        shift = shift % a.shape[0]
        return a if shift == 0 else pltpu.roll(a, shift, 0)

    def group(a, shift):
        by = lax.broadcasted_iota(jnp.int32, a.shape, 0) % gy
        shift = shift % gy
        if shift == 0:
            return a
        return jnp.where(by < gy - shift, turn(a, -shift), turn(a, gy - shift))

    def circulant(coef, a, move, count):
        value = coef(0) * a
        for d in range(1, count // 2 + 1):
            near = move(a, d) if 2 * d == count else move(a, d) + move(a, -d)
            value = value + coef(d) * near
        return value

    def solve_x(jump, step):
        return circulant(lambda d: tabs["gap_x"][d : d + 1, :], jump, lambda a, d: turn(a, -d * step), gx)

    def spread(minus, plus, table, width):
        count = minus.shape[0]
        both = dot(jnp.concatenate([minus, plus], axis=0), table)
        lane = lax.broadcasted_iota(jnp.int32, (count, both.shape[1]), 1)
        return jnp.where(lane < width, -both[:count], both[count:])

    flux = solve_x(t_even - t_odd - turn(t_even + t_odd, -gy), gy)
    minus, plus = flux - turn(flux, gy), flux + turn(flux, gy)
    s_even = s_even + spread(minus[:, :hy], plus[:, :hy], tabs["cross_t"][:hy, :], hx)
    s_odd = s_odd + spread(minus[:, hy:], plus[:, hy:], tabs["cross_t"][hy:, :], hx)
    jump = s_even - s_odd - group(s_even + s_odd, 1)
    lines = dot(tabs["gather"][...], dot(jump, tabs["cos_x"][...]))
    rows = lines.shape[0] // 2
    real, imag = lines[:rows], lines[rows:]
    cosine, sine = tabs["twist"][0], tabs["twist"][1]
    turned = jnp.concatenate([real * cosine + imag * sine, imag * cosine - real * sine], axis=0)
    both = dot(turned, tabs["fourier"][...])
    waves = jnp.concatenate(
        [both[:rows, :lx] + both[rows:, lx:], both[rows:, :lx] - both[:rows, lx:]], axis=0
    )
    waves = circulant(lambda d: tabs["gap_y"][d], waves, group, gy)
    both = dot(waves, tabs["fourier"][...])
    real = both[:rows, :lx] - both[rows:, lx:]
    imag = both[:rows, lx:] + both[rows:, :lx]
    turned = jnp.concatenate([real * cosine - imag * sine, real * sine + imag * cosine], axis=0)
    flow = dot(dot(tabs["scatter"][...], turned), tabs["cos_xt"][...])
    flow_minus, flow_plus = flow - group(flow, -1), flow + group(flow, -1)
    row = lax.broadcasted_iota(jnp.int32, (gx, blocks), 0)
    col = lax.broadcasted_iota(jnp.int32, (gx, blocks), 1)
    pick = jnp.where(col == row * gy + place[0], 1.0, 0.0).astype(F32)
    chosen = dot(pick, jnp.concatenate([t_even, t_odd, flow_minus, flow_plus], axis=1))
    t_even, t_odd = chosen[:, :ly], chosen[:, ly : 2 * ly]
    minus, plus = chosen[:, 2 * ly : 2 * ly + lx], chosen[:, 2 * ly + lx :]
    t_even = t_even + spread(minus[:, :hx], plus[:, :hx], tabs["cross"][:hx, :], hy)
    t_odd = t_odd + spread(minus[:, hx:], plus[:, hx:], tabs["cross"][hx:, :], hy)
    flux = solve_x(t_even - t_odd - turn(t_even + t_odd, -1), 1)
    line = jnp.concatenate([turn(flux, 1) - flux, flux + turn(flux, 1), -minus, plus], axis=1)
    for j in range(line.shape[1] // 128):
        out[:, j, :] = line[:, j * 128 : (j + 1) * 128]
    total = jnp.sum(jnp.sum(pay[:, nrow, :], axis=0, keepdims=True), axis=1, keepdims=True)
    out[:, nrow, :] = jnp.broadcast_to(total, (gx, 128))


def finish_kernel(nrow, sums, corr, beta_in, state, z1, z2, out):
    beta_sq = beta_in[0, nrow : nrow + 1, :]
    top_left = corr[0, nrow : nrow + 1, :] / beta_sq
    beta = jnp.sqrt(beta_sq)
    total = jnp.sum(jnp.sum(sums[...], axis=0), axis=1, keepdims=True)
    total = jnp.broadcast_to(total, (8, 128))
    length_sq, cross, first, image_sq = [total[n : n + 1, :] for n in range(4)]
    length = jnp.sqrt(length_sq)
    below_first = length / beta
    top_right = first / (beta * length)
    middle_right = cross / length_sq
    bottom_sq = image_sq / length_sq - top_right * top_right - middle_right * middle_right
    first_radius = jnp.sqrt(top_left * top_left + below_first * below_first)
    first_cosine = top_left / first_radius
    first_sine = below_first / first_radius
    upper_right = first_cosine * top_right + first_sine * middle_right
    lower_right = -first_sine * top_right + first_cosine * middle_right
    lower_target = -first_sine * beta
    second_coef = lower_right * lower_target / (lower_right * lower_right + jnp.maximum(bottom_sq, 0.0))
    first_coef = (first_cosine * beta - upper_right * second_coef) / first_radius
    a = (first_coef / beta)[:, :1]
    b = (second_coef / length)[:, :1]
    for k in range(out.shape[2]):
        out[:, 0, k, :] = state[:, 0, k, :] + (a * z1[k] + b * z2[k])


def halo(state):
    def shift(cells, axis, step):
        count = lax.axis_size(axis)
        return lax.ppermute(cells, axis, [(i, (i + step) % count) for i in range(count)])

    lo = shift(state[-1:], "gx", 1)
    hi = shift(state[:1], "gx", -1)
    column = lambda cells: jnp.transpose(cells[:, 0, :, 0], (1, 0))
    left = shift(column(state[..., -1:]), "gy", 1)
    right = shift(column(state[..., :1]), "gy", -1)
    return lo, hi, jnp.stack([left, right], axis=2)


def body(gx, gy, state, mobility):
    lx, _, kinds, ly = state.shape
    main, face = make_tables(lx, ly, gx, gy)
    main = {name: jnp.asarray(table) for name, table in main.items()}
    face = {name: jnp.asarray(table) for name, table in face.items()}
    nrow = (2 * lx + 2 * ly) // 128
    width = -(-(nrow + 1) // 8) * 8
    vmem = pl.BlockSpec(memory_space=pltpu.VMEM)
    hbm = pl.BlockSpec(memory_space=pl.ANY)
    smem = pl.BlockSpec(memory_space=pltpu.SMEM)
    params = pltpu.CompilerParams(vmem_limit_bytes=VMEM_LIMIT)
    whole = jax.ShapeDtypeStruct((kinds, lx, ly), F32)
    payload = jax.ShapeDtypeStruct((gx * gy, width, 128), F32)
    full = pltpu.VMEM((kinds, lx, ly), F32)
    plane = pltpu.VMEM((lx, ly), F32)
    dma = pltpu.SemaphoreType.DMA
    place = lax.axis_index("gy").astype(jnp.int32).reshape(1)

    def faces(pay):
        pay = lax.all_to_all(pay, ("gx", "gy"), split_axis=0, concat_axis=0, tiled=True)
        fluxes = pl.pallas_call(
            functools.partial(face_kernel, gx, gy, lx, ly, nrow),
            out_shape=jax.ShapeDtypeStruct((gx, width, 128), F32),
            in_specs=[smem, vmem] + [vmem] * len(FACE),
            out_specs=vmem,
            compiler_params=params,
            name="faces",
        )(place, pay, *[face[name] for name in FACE])
        return lax.all_to_all(fluxes, "gx", split_axis=0, concat_axis=0, tiled=True)

    lo, hi, side = halo(state)
    names = ("fwd_y", "fwd_x", "inverse", "edge_x", "edge_y")
    r0, spec, pay = pl.pallas_call(
        functools.partial(start_kernel, gx, gy, nrow),
        out_shape=(whole, whole, payload),
        in_specs=[hbm, hbm, vmem, vmem, vmem] + [vmem] * len(names),
        out_specs=(hbm, hbm, vmem),
        scratch_shapes=[
            pltpu.VMEM((kinds, lx + 16, ly), F32),
            plane,
            full,
            full,
            pltpu.VMEM((8, 128), F32),
            dma((kinds + 1,)),
            dma((2,)),
        ],
        compiler_params=params,
        name="start",
    )(state, mobility, lo, hi, side, *[main[name] for name in names])
    corr_one = faces(pay)
    z1, q1, spec, pay = pl.pallas_call(
        functools.partial(middle_kernel, gx, gy, nrow),
        out_shape=(whole, whole, whole, payload),
        in_specs=[vmem, hbm, hbm, hbm, hbm] + [vmem] * len(MAIN),
        out_specs=(hbm, hbm, hbm, vmem),
        scratch_shapes=[
            full,
            plane,
            full,
            full,
            full,
            pltpu.VMEM((8, 128), F32),
            dma((kinds + 3,)),
            dma((3,)),
        ],
        compiler_params=params,
        name="middle",
    )(corr_one, state, mobility, spec, r0, *[main[name] for name in MAIN])
    corr_two = faces(pay)
    names = ("inv_y", "inv_x", "inverse", "ends_x", "ends_y")
    z2, sums = pl.pallas_call(
        functools.partial(last_kernel, gx, gy, nrow),
        out_shape=(whole, jax.ShapeDtypeStruct((gx * gy, 8, 128), F32)),
        in_specs=[vmem, vmem] + [hbm] * 6 + [vmem] * len(names),
        out_specs=(hbm, vmem),
        scratch_shapes=[
            full,
            plane,
            full,
            full,
            full,
            full,
            pltpu.VMEM((4, 8, 128), F32),
            dma((kinds + 5,)),
            dma((1,)),
        ],
        compiler_params=params,
        name="last",
    )(corr_two, corr_one, state, mobility, spec, r0, q1, z1, *[main[name] for name in names])
    sums = lax.all_to_all(sums, ("gx", "gy"), split_axis=0, concat_axis=0, tiled=True)
    step = 32
    corr_spec = pl.BlockSpec(corr_one.shape, lambda i: (0, 0, 0))
    return pl.pallas_call(
        functools.partial(finish_kernel, nrow),
        grid=(lx // step,),
        out_shape=jax.ShapeDtypeStruct(state.shape, F32),
        in_specs=[
            pl.BlockSpec(sums.shape, lambda i: (0, 0, 0)),
            corr_spec,
            corr_spec,
            pl.BlockSpec((step, 1, kinds, ly), lambda i: (i, 0, 0, 0)),
            pl.BlockSpec((kinds, step, ly), lambda i: (0, i, 0)),
            pl.BlockSpec((kinds, step, ly), lambda i: (0, i, 0)),
        ],
        out_specs=pl.BlockSpec((step, 1, kinds, ly), lambda i: (i, 0, 0, 0)),
        compiler_params=params,
        name="finish",
    )(sums, corr_two, corr_one, state, z1, z2)


def solution(mesh):
    return jax.shard_map(
        functools.partial(body, mesh.shape["gx"], mesh.shape["gy"]),
        mesh=mesh,
        in_specs=(P("gx", None, None, "gy"), P("gx", None, "gy")),
        out_specs=P("gx", None, None, "gy"),
        check_vma=False,
    )
```

time: 2170 us -> 167 us (0.08)
  blocking collectives: 694 us -> 47.1 us
  other arithmetic: 568 us -> 0.01 us
  matrix products: 368 us -> 0 us
  local copies, waits for them, and re-layouts: 363 us -> 6.04 us
  Pallas kernels: 0 us -> 87.6 us
  waiting for transfers between devices: 103 us -> 15.7 us
  starting transfers between devices: 52.2 us -> 9.6 us
    all_to_all x6 -> x4, blocking collectives: 498 us -> 47.1 us  [the longest x2 21.7 us: faces(): return lax.all_to_all(fluxes, 'gx', split_axis=0, concat_axis=0, tiled=True)]
    dot_general x8 -> x0, other arithmetic: 405 us -> none  [the longest x2 134 us: precondition(): jnp.dot(x_table, flat, precision=highest, preferred_element_type=jnp.floa...]
    dot_general x8 -> x0, matrix products: 368 us -> none  [the longest x2 189 us: precondition(): lax.dot_general(scaled.reshape(-1, cols_total), y_table, (((1,), (1,)), (...]
    psum x5 -> x0, blocking collectives: 196 us -> none  [the longest x3 122 us: length(): return lax.psum(jnp.sum(vector * vector), ('gx', 'gy'))]
    all_to_all x27 -> x0, local copies, waits for them, and re-layouts: 135 us -> none  [the longest x6 37.5 us: precondition(): lax.all_to_all(back_rows, 'gy', split_axis=3, concat_axis=0, tiled=True)]
    unnamed x61 -> x8, local copies, waits for them, and re-layouts: 134 us -> 2.06 us
    all_to_all x6 -> x1, waiting for transfers between devices: 103 us -> 10.6 us  [faces(): lax.all_to_all(pay, ('gx', 'gy'), split_axis=0, concat_axis=0, tiled=True)]
    pallas_call x0 -> x6, Pallas kernels: none -> 87.6 us  [the longest x1 26.9 us: body(): pl.pallas_call(functools.partial(middle_kernel, gx, gy, nrow), out_shape=...]
  transfers between devices with their start and end apart: 18 -> 5, of which waited for: 4 -> 3; matrix products, arithmetic and copies ran while one was open for 20% -> 1% of each run, Pallas kernels for 0% -> 0%
where the time goes in v1:
time: 167 us; the launch traced here: 166 us
  Pallas kernels  87.6 us (52%)
  blocking collectives  47.1 us (28%)
  waiting for transfers between devices  15.7 us (9%)
  starting transfers between devices  9.6 us (6%)
  local copies, waits for them, and re-layouts  6.04 us (4%)
    pallas_call x1, Pallas kernels, body(): pl.pallas_call(functools.partial(middle_kernel, gx, gy, nrow), out_shape=...  26.9 us
    pallas_call x1, Pallas kernels, body(): pl.pallas_call(functools.partial(start_kernel, gx, gy, nrow), out_shape=(...  22 us
    all_to_all x2, blocking collectives, faces(): return lax.all_to_all(fluxes, 'gx', split_axis=0, concat_axis=0, tiled=True)  21.7 us
    pallas_call x1, Pallas kernels, body(): pl.pallas_call(functools.partial(last_kernel, gx, gy, nrow), out_shape=(w...  18.1 us
    all_to_all x1, blocking collectives, faces(): lax.all_to_all(pay, ('gx', 'gy'), split_axis=0, concat_axis=0, tiled=True)  13.9 us
    all_to_all x1, blocking collectives, body(): lax.all_to_all(sums, ('gx', 'gy'), split_axis=0, concat_axis=0, tiled=True)  11.5 us
    pallas_call x2, Pallas kernels, faces(): pl.pallas_call(functools.partial(face_kernel, gx, gy, lx, ly, nrow), out_...  10.7 us
    all_to_all x1, waiting for transfers between devices, faces(): lax.all_to_all(pay, ('gx', 'gy'), split_axis=0, concat_axis=0, tiled=True)  10.6 us
  transfers between devices with their start and end apart: 5, of which 3 were waited for; matrix products, arithmetic and copies ran while one was open for 1% of the time, Pallas kernels for 0%

profile of v1, /device:TPU:0, one launch (start us, length us, event | category | flops | bytes accessed | tf_op | source)
XLA Modules:
  0.0 166.1 jit_solution(6932286820005123286)
XLA Ops:
  0.0 1.9 %fusion = (f32[256,1,8,1]{3,2,1,0:T(8,128)S(1)}, f32[256,1,8,1]{3,2,1,0:T(8,128)S(1)}) fusion(f32[256,1,8,512]{3,2,1,0:T(8,128)} %state.1), kind=kLoop, calls=%fused_computation.1 | loop fusion | bytes 32768 | tf_op jit(solution)/shard_map/slice | solution.py:530
  1.9 0.4 copy.32
  2.3 2.4 %collective-permute-start.3 = (f32[8,256]{1,0:T(8,128)S(1)}, f32[8,256]{1,0:T(8,128)S(1)}, u32[]{:S(2)}, u32[]{:S(2)}) collective-permute-start(f32[8,256]{1,0:T(8,128)S(1)} %bitcast.9), channel_id=1, source_target_pairs={{0,3},{1,0},{2,1},{3,2},{4,7},{5,4},{6,5},{7,6},{8,11},{9,8},{10,9... | collective-permute-start | bytes 24584 | tf_op jit(solution)/shard_map/ppermute | solution.py:525
  4.7 0.4 copy.31
  5.1 0.0 collective-permute-start.2
  5.1 0.7 fusion.1
  5.8 4.6 %collective-permute-start.1 = (f32[1,1,8,512]{3,2,1,0:T(8,128)S(1)}, f32[1,1,8,512]{3,2,1,0:T(8,128)S(1)}, u32[]{:S(2)}, u32[]{:S(2)}) collective-permute-start(f32[1,1,8,512]{3,2,1,0:T(8,128)S(1)} %get-tuple-element.25), channel_id=1, source_target_pairs={{0,28},{4,0},{8,4},{12,8},{16,12},{20,16},{24,20},{28,24},{1,29},{... | collective-permute-start | bytes 49160 | tf_op jit(solution)/shard_map/ppermute | solution.py:525
  10.4 0.0 collective-permute-start
  10.4 0.0 collective-permute-done.3
  10.4 0.0 collective-permute-done.2
  10.4 1.3 copy.30.refs_4_
  11.8 0.1 collective-permute-done.1.refs_3_
  11.8 0.0 copy-start.1
  11.8 5.0 %collective-permute-done.refs_2_ = f32[1,1,8,512]{3,2,1,0:T(8,128)S(1)} collective-permute-done((f32[1,1,8,512]{3,2,1,0:T(8,128)S(1)}, f32[1,1,8,512]{3,2,1,0:T(8,128)S(1)}, u32[]{:S(2)}, u32[]{:S(2)}) %collective-permute-start) | collective-permute-done | bytes 16416 | tf_op jit(solution)/shard_map/ppermute | solution.py:525
  16.9 0.0 copy-done.1
  16.9 0.0 copy-start.2
  16.9 0.6 copy-done.2
  17.5 22.0 %start.1 = (f32[8,256,512]{2,1,0:T(8,128)}, f32[8,256,512]{2,1,0:T(8,128)}, f32[32,16,128]{2,1,0:T(8,128)}) custom-call(f32[256,1,8,512]{3,2,1,0:T(8,128)} %state.1, f32[256,1,512]{2,1,0:T(1,128)} %refs_3_.3, f32[1,1,8,512]{3,2,1,0:T(8,128)} %copy-done.2, f32[1,1,8,512]{3,2,1,0:T(8,128)} %copy-done.1, f32[8,256,2]{2,1,0:T(8,128)} %copy.30.refs_4_, ...), custom_call_target="tpu_custom_call" | custom-call | tf_op jit(solution)/shard_map/start/pallas_call | solution.py:567
  39.4 2.6 %all-to-all-start = ((f32[32,16,128]{2,1,0:T(8,128)}), f32[32,16,128]{2,1,0:T(8,128)S(1)}, u32[]{:S(2)}, u32[]{:S(2)}) async-start(f32[32,16,128]{2,1,0:T(8,128)} %get-tuple-element.14), calls=%async_computation | async-start | bytes 524288 | tf_op jit(solution)/shard_map/all_to_all | solution.py:554
  42.1 10.6 %all-to-all-done.pay = f32[32,16,128]{2,1,0:T(8,128)S(1)} async-done(((f32[32,16,128]{2,1,0:T(8,128)}), f32[32,16,128]{2,1,0:T(8,128)S(1)}, u32[]{:S(2)}, u32[]{:S(2)}) %all-to-all-start) | async-done | bytes 262176 | tf_op jit(solution)/shard_map/all_to_all | solution.py:554
  52.6 0.0 copy-start
  52.6 0.7 copy-done
  53.3 5.3 %faces.2 = f32[8,16,128]{2,1,0:T(8,128)} custom-call(s32[1]{0:T(128)} %bitcast.place, f32[32,16,128]{2,1,0:T(8,128)} %copy-done, f32[256,512]{1,0:T(8,128)} %constant.51.clone.refs_0_, f32[512,256]{1,0:T(8,128)} %constant.52.clone.refs_1_, f32[256,256]{1,0:T(8,128)} %constant.53.clone.refs_2_, f32[256,256]{1,0:T(8,128)} %constant.54.clone.refs_3_, ...), custom_call_target="tpu_custom_call" | custom-call | tf_op jit(solution)/shard_map/faces/pallas_call | solution.py:555
  58.7 10.9 %all_to_all.25.refs_0_.refs_1_.beta_in = f32[8,16,128]{2,1,0:T(8,128)} all-to-all(f32[8,16,128]{2,1,0:T(8,128)} %faces.2), channel_id=1, replica_groups=mesh['gx'=8,'gy'=4] {'gx'}, dimensions={0} | all-to-all | bytes 131072 | tf_op jit(solution)/shard_map/all_to_all | solution.py:563
  69.5 26.9 %middle.1 = (f32[8,256,512]{2,1,0:T(8,128)}, f32[8,256,512]{2,1,0:T(8,128)}, f32[8,256,512]{2,1,0:T(8,128)}, f32[32,16,128]{2,1,0:T(8,128)}) custom-call(f32[8,16,128]{2,1,0:T(8,128)} %all_to_all.25.refs_0_.refs_1_.beta_in, f32[256,1,8,512]{3,2,1,0:T(8,128)} %state.1, f32[256,1,512]{2,1,0:T(1,128)} %refs_3_.3, f32[8,256,512]{2,1,0:T(8,128)} %get-tuple-element.15.refs_3_, ...), custom_call_target="tpu_custom_call" | custom-call | tf_op jit(solution)/shard_map/middle/pallas_call | solution.py:585
  96.5 13.9 %all_to_all.26.pay = f32[32,16,128]{2,1,0:T(8,128)} all-to-all(f32[32,16,128]{2,1,0:T(8,128)} %get-tuple-element.17), channel_id=1, replica_groups=mesh['gx'=8,'gy'=4] {'gx','gy'}, dimensions={0} | all-to-all | bytes 524288 | tf_op jit(solution)/shard_map/all_to_all | solution.py:554
  110.3 5.3 %faces.3 = f32[8,16,128]{2,1,0:T(8,128)} custom-call(s32[1]{0:T(128)} %bitcast.place, f32[32,16,128]{2,1,0:T(8,128)} %all_to_all.26.pay, f32[256,512]{1,0:T(8,128)} %constant.51.clone.refs_0_, f32[512,256]{1,0:T(8,128)} %constant.52.clone.refs_1_, f32[256,256]{1,0:T(8,128)} %constant.53.clone.refs_2_, f32[256,256]{1,0:T(8,128)} %constant.54.clone.refs_3_, ...), custom_call_target="tpu_custom_call" | custom-call | tf_op jit(solution)/shard_map/faces/pallas_call | solution.py:555
  115.7 10.9 %all_to_all.27.refs_0_.corr = f32[8,16,128]{2,1,0:T(8,128)} all-to-all(f32[8,16,128]{2,1,0:T(8,128)} %faces.3), channel_id=1, replica_groups=mesh['gx'=8,'gy'=4] {'gx'}, dimensions={0} | all-to-all | bytes 131072 | tf_op jit(solution)/shard_map/all_to_all | solution.py:563
  126.6 18.1 %last.1 = (f32[8,256,512]{2,1,0:T(8,128)}, f32[32,8,128]{2,1,0:T(8,128)}) custom-call(f32[8,16,128]{2,1,0:T(8,128)} %all_to_all.27.refs_0_.corr, f32[8,16,128]{2,1,0:T(8,128)} %all_to_all.25.refs_0_.refs_1_.beta_in, f32[256,1,8,512]{3,2,1,0:T(8,128)} %state.1, f32[256,1,512]{2,1,0:T(1,128)} %refs_3_.3, f32[8,256,512]{2,1,0:T(8,128)} %get-tuple-element.18.refs_4_, ...), custom_call_target="tpu_custom_call" | custom-call | tf_op jit(solution)/shard_map/last/pallas_call | solution.py:605
  144.7 11.5 %all_to_all.28.sums = f32[32,8,128]{2,1,0:T(8,128)} all-to-all(f32[32,8,128]{2,1,0:T(8,128)} %get-tuple-element.21), channel_id=1, replica_groups=mesh['gx'=8,'gy'=4] {'gx','gy'}, dimensions={0} | all-to-all | bytes 262144 | tf_op jit(solution)/shard_map/all_to_all | solution.py:624
  156.2 9.9 %finish.1 = f32[256,1,8,512]{3,2,1,0:T(8,128)} custom-call(f32[32,8,128]{2,1,0:T(8,128)} %all_to_all.28.sums, f32[8,16,128]{2,1,0:T(8,128)} %all_to_all.27.refs_0_.corr, f32[8,16,128]{2,1,0:T(8,128)} %all_to_all.25.refs_0_.refs_1_.beta_in, f32[256,1,8,512]{3,2,1,0:T(8,128)} %state.1, f32[8,256,512]{2,1,0:T(8,128)} %get-tuple-element.20.refs_7_.z1, ...), custom_call_target="tpu_custom_call" | custom-call | tf_op jit(solution)/shard_map/finish/pallas_call | solution.py:627
  (1 shorter events, 0.0 us)
Async XLA Ops:
  2.3 8.1 %collective-permute-start.3 = (f32[8,256]{1,0:T(8,128)S(1)}, f32[8,256]{1,0:T(8,128)S(1)}, u32[]{:S(2)}, u32[]{:S(2)}) collective-permute-start(f32[8,256]{1,0:T(8,128)S(1)} %bitcast.9), channel_id=1, source_target_pairs={{0,3},{1,0},{2,1},{3,2},{4,7},{5,4},{6,5},{7,6},{8,11},{9,8},{10,9... | collective-permute-start | bytes 24584 | tf_op jit(solution)/shard_map/ppermute | solution.py:525
  5.1 5.4 %collective-permute-start.2 = (f32[8,256]{1,0:T(8,128)S(1)}, f32[8,256]{1,0:T(8,128)S(1)}, u32[]{:S(2)}, u32[]{:S(2)}) collective-permute-start(f32[8,256]{1,0:T(8,128)S(1)} %bitcast.10), channel_id=1, source_target_pairs={{0,1},{1,2},{2,3},{3,0},{4,5},{5,6},{6,7},{7,4},{8,9},{9,10},{10,1... | collective-permute-start | bytes 24584 | tf_op jit(solution)/shard_map/ppermute | solution.py:525
  5.8 6.0 %collective-permute-start.1 = (f32[1,1,8,512]{3,2,1,0:T(8,128)S(1)}, f32[1,1,8,512]{3,2,1,0:T(8,128)S(1)}, u32[]{:S(2)}, u32[]{:S(2)}) collective-permute-start(f32[1,1,8,512]{3,2,1,0:T(8,128)S(1)} %get-tuple-element.25), channel_id=1, source_target_pairs={{0,28},{4,0},{8,4},{12,8},{16,12},{20,16},{24,20},{28,24},{1,29},{... | collective-permute-start | bytes 49160 | tf_op jit(solution)/shard_map/ppermute | solution.py:525
  10.4 6.5 %collective-permute-start = (f32[1,1,8,512]{3,2,1,0:T(8,128)S(1)}, f32[1,1,8,512]{3,2,1,0:T(8,128)S(1)}, u32[]{:S(2)}, u32[]{:S(2)}) collective-permute-start(f32[1,1,8,512]{3,2,1,0:T(8,128)S(1)} %get-tuple-element.26), channel_id=1, source_target_pairs={{0,4},{4,8},{8,12},{12,16},{16,20},{20,24},{24,28},{28,0},{1,5},{5... | collective-permute-start | bytes 49160 | tf_op jit(solution)/shard_map/ppermute | solution.py:525
  11.8 5.0 %copy-start.1 = (f32[1,1,8,512]{3,2,1,0:T(8,128)}, f32[1,1,8,512]{3,2,1,0:T(8,128)S(1)}, u32[]{:S(2)}) copy-start(f32[1,1,8,512]{3,2,1,0:T(8,128)S(1)} %collective-permute-done.1.refs_3_) | copy-start | bytes 49156
  16.9 0.6 copy-start.2
  39.4 13.2 %all-to-all-start = ((f32[32,16,128]{2,1,0:T(8,128)}), f32[32,16,128]{2,1,0:T(8,128)S(1)}, u32[]{:S(2)}, u32[]{:S(2)}) async-start(f32[32,16,128]{2,1,0:T(8,128)} %get-tuple-element.14), calls=%async_computation | async-start | bytes 524288 | tf_op jit(solution)/shard_map/all_to_all | solution.py:554
  52.6 0.7 copy-start

commit v2 on v1

v2 whole, which is shorter than its diff:
```python
import functools
import math

import jax
import jax.numpy as jnp
import numpy as np
from jax import lax
from jax.experimental import pallas as pl
from jax.experimental.pallas import tpu as pltpu
from jax.sharding import PartitionSpec as P

linear_coef = 1.0
cubic_coef = 1.0
cross_coef = 1.5
gradient_coef = 200.0
time_step = 200.0
stiffness = time_step * gradient_coef

F32 = jnp.float32
BF16 = jnp.bfloat16
GRANTS = dict(edges=56, start=20, rim=8, faces=8, middle=16, last=16, finish=8)


def cosine_table(size):
    modes = np.arange(size)[:, None]
    cells = np.arange(size)[None, :]
    table = np.sqrt(2.0 / size) * np.cos(np.pi * modes * (cells + 0.5) / size)
    table[0] = np.sqrt(1.0 / size)
    values = 4.0 * np.sin(np.pi * np.arange(size) / (2 * size)) ** 2
    order = np.concatenate([np.arange(0, size, 2), np.arange(1, size, 2)])
    return table[order], values[order]


def split_const(table):
    high = table.astype(np.float32).astype(jnp.bfloat16)
    low = (table - high.astype(np.float64)).astype(np.float32).astype(jnp.bfloat16)
    return high, low


def right_const(table):
    high, low = split_const(table)
    return np.concatenate([high, low, high], axis=0)


def left_const(table):
    high, low = split_const(table)
    return np.concatenate([high, low, high], axis=1)


def make_tables(lx, ly, gx, gy):
    cos_x, value_x = cosine_table(lx)
    cos_y, value_y = cosine_table(ly)
    edge_x, edge_y = cos_x[:, 0], cos_y[:, 0]
    inverse = 1.0 / (1.0 + stiffness * (value_x[:, None] + value_y[None, :]))
    cross = edge_x[:, None] * edge_y[None, :] * inverse
    sign_x = np.where(np.arange(lx) < lx // 2, 1.0, -1.0)
    sign_y = np.where(np.arange(ly) < ly // 2, 1.0, -1.0)
    own = (edge_x[:, None] ** 2 * inverse).sum(0)
    other = (sign_x[:, None] * edge_x[:, None] ** 2 * inverse).sum(0)
    wave = np.arange(gx)
    eigen = 1.0 / stiffness + 2.0 * own[None] - 2.0 * other[None] * np.cos(2 * np.pi * wave / gx)[:, None]
    gap_x = np.stack(
        [(np.cos(2 * np.pi * wave * d / gx)[:, None] / eigen).mean(0) for d in range(gx // 2 + 1)]
    )
    total = lx * gx
    half = gx // 2 + 1
    rows = -(-half * gy // 8) * 8
    freq = gx * np.arange(lx)[None, :] + np.arange(half)[:, None]
    symbol = 1.0 + stiffness * (4.0 * np.sin(np.pi * freq / total) ** 2)[:, :, None] + stiffness * value_y
    own = (edge_y**2 / symbol).sum(-1)
    other = (sign_y * edge_y**2 / symbol).sum(-1)
    wave = np.arange(gy)
    eigen = 1.0 / stiffness + 2.0 * own[None] - 2.0 * other[None] * np.cos(2 * np.pi * wave / gy)[:, None, None]
    gap_y = np.zeros((gy // 2 + 1, 2 * rows, lx))
    for d in range(gy // 2 + 1):
        coef = (np.cos(2 * np.pi * wave * d / gy)[:, None, None] / eigen).mean(0)
        coef = np.repeat(coef, gy, axis=0)
        gap_y[d, : half * gy] = coef
        gap_y[d, rows : rows + half * gy] = coef
    cells = np.arange(lx)
    angle = 2 * np.pi * np.outer(cells, cells) / lx
    fourier = np.concatenate([np.cos(angle), np.sin(angle)], axis=1)
    twist = np.zeros((2, rows, lx))
    gather = np.zeros((2 * rows, gx * gy))
    scatter = np.zeros((gx * gy, 2 * rows))
    for q in range(half):
        theta = 2 * np.pi * q * cells / total
        weight = (1.0 if q in (0, gx // 2) else 2.0) / total
        for j in range(gy):
            twist[0, q * gy + j] = np.cos(theta)
            twist[1, q * gy + j] = np.sin(theta)
            for i in range(gx):
                phase = 2 * np.pi * q * i / gx
                gather[q * gy + j, i * gy + j] = np.cos(phase)
                gather[rows + q * gy + j, i * gy + j] = -np.sin(phase)
                scatter[i * gy + j, q * gy + j] = weight * np.cos(phase)
                scatter[i * gy + j, rows + q * gy + j] = -weight * np.sin(phase)
    single = lambda a: np.ascontiguousarray(a, dtype=np.float32)
    zero_x, zero_y = np.zeros(lx // 2), np.zeros(ly // 2)
    ends_x = np.zeros((8, lx))
    ends_x[0], ends_x[1] = (
        np.concatenate([edge_x[: lx // 2], zero_x]),
        np.concatenate([zero_x, edge_x[lx // 2 :]]),
    )
    ends_y = np.zeros((8, ly))
    ends_y[2], ends_y[3] = (
        np.concatenate([edge_y[: ly // 2], zero_y]),
        np.concatenate([zero_y, edge_y[ly // 2 :]]),
    )
    main = dict(
        fwd_ye=right_const(cos_y[: ly // 2, : ly // 2].T),
        fwd_yo=right_const(cos_y[ly // 2 :, : ly // 2].T),
        fwd_x=left_const(cos_x),
        inv_ye=right_const(cos_y[: ly // 2, : ly // 2]),
        inv_yo=right_const(cos_y[ly // 2 :, : ly // 2]),
        inv_x=left_const(cos_x.T),
        inverse=single(inverse),
        edge_x=single(np.repeat(edge_x[:, None], 128, axis=1)),
        edge_y=single(np.repeat(edge_y[None, :], 8, axis=0)),
        ends_x=single(ends_x),
        ends_y=single(ends_y),
    )
    face = dict(
        cross=single(cross),
        cross_t=single(cross.T),
        cos_x=single(cos_x),
        cos_xt=single(cos_x.T),
        gap_x=single(gap_x),
        gap_y=single(gap_y.reshape(-1, lx)),
        fourier=single(fourier),
        twist=single(twist.reshape(-1, lx)),
        gather=single(gather),
        scatter=single(scatter),
        self_x=single(np.stack([(edge_x[:, None] ** 2 * inverse)[h].sum(0) for h in np.split(np.arange(lx), 2)])),
        self_y=single(np.stack([(edge_y**2 * inverse)[:, h].sum(1) for h in np.split(np.arange(ly), 2)])),
    )
    return main, face


def packed(tables):
    arrays, places = [], []
    for kind, step in ((np.dtype(np.float32), 8), (np.dtype(jnp.bfloat16), 16)):
        strips, start = [], 0
        for name, table in tables.items():
            if table.dtype != kind:
                continue
            rows, cols = -(-table.shape[0] // step) * step, -(-table.shape[1] // 128) * 128
            wide = np.zeros((rows, cols), kind)
            wide[: table.shape[0], : table.shape[1]] = table
            for j in range(cols // 128):
                strips.append(wide[:, j * 128 : (j + 1) * 128])
                places.append((name, len(arrays), start, rows, j, cols))
                start += rows
        arrays.append(np.concatenate(strips, axis=0))
    return arrays, places


def halves(x):
    high = x.astype(BF16)
    low = (x - high.astype(F32)).astype(BF16)
    return high, low


def times_right(x, const):
    high, low = halves(x)
    return jnp.dot(jnp.concatenate([high, high, low], axis=1), const[...], preferred_element_type=F32)


def times_left(const, x):
    high, low = halves(x)
    return jnp.dot(const[...], jnp.concatenate([high, high, low], axis=0), preferred_element_type=F32)


def thirds(x):
    high = x.astype(BF16).astype(F32)
    rest = x - high
    mid = rest.astype(BF16).astype(F32)
    return high, mid, rest - mid


def outer_sum(a, b):
    ah, am, al = thirds(a)
    bh, bm, bl = thirds(b)
    left = jnp.concatenate([ah, ah, am, am, ah, al], axis=0).astype(BF16)
    right = jnp.concatenate([bh, bm, bh, bm, bl, bh], axis=0).astype(BF16)
    return lax.dot_general(left, right, (((0,), (0,)), ((), ())), preferred_element_type=F32)


def flipped(x):
    place = 127 - lax.broadcasted_iota(jnp.int32, (x.shape[0], 128), 1)
    tiles = [x[:, j * 128 : (j + 1) * 128] for j in range(x.shape[1] // 128)]
    return jnp.concatenate(
        [jnp.take_along_axis(tile, place, axis=1, mode="promise_in_bounds") for tile in tiles[::-1]], axis=1
    )


def lines_out(x, tabs):
    half = x.shape[1] // 2
    left, right = x[:, :half], flipped(x[:, half:])
    return jnp.concatenate(
        [times_right(left + right, tabs["fwd_ye"]), times_right(left - right, tabs["fwd_yo"])], axis=1
    )


def lines_back(x, tabs):
    half = x.shape[1] // 2
    even = times_right(x[:, :half], tabs["inv_ye"])
    odd = times_right(x[:, half:], tabs["inv_yo"])
    return jnp.concatenate([even + odd, flipped(even - odd)], axis=1)


def modes_out(lines, group, spec, tabs, store):
    lx, ly = spec.shape[1:]
    hat = times_left(tabs["fwd_x"], jnp.concatenate(lines, axis=1))
    for i, k in enumerate(group):
        spectrum = hat[:, i * ly : (i + 1) * ly] * tabs["inverse"][...]
        spec[k] = spectrum
        weighted = spectrum * tabs["edge_x"][:, :1]
        top = [
            jnp.sum(weighted[: lx // 2], axis=0, keepdims=True),
            jnp.sum(weighted[lx // 2 :], axis=0, keepdims=True),
        ]
        weighted = spectrum * tabs["edge_y"][:1, :]
        cols = [weighted[:, j * 128 : (j + 1) * 128] for j in range(ly // 128)]
        half = len(cols) // 2
        folded = jnp.concatenate([sum(cols[1:half], cols[0]), sum(cols[half + 1 :], cols[half])], axis=0)
        high, low = halves(folded)
        side = lax.dot_general(
            jnp.ones((8, 256), BF16),
            jnp.concatenate([high, low], axis=1),
            (((1,), (1,)), ((), ())),
            preferred_element_type=F32,
        )[:1]
        store(k, jnp.concatenate([*top, side], axis=1))


def row_piece(ref, k, start, count):
    return jnp.concatenate([ref[k, start + j : start + j + 1, :] for j in range(count)], axis=1)


def transform_back(spec, group, corrs, tabs):
    lx, ly = spec.shape[1:]
    nx, ny = lx // 128, ly // 128
    row = lax.broadcasted_iota(jnp.int32, (8, 1), 0)
    spectra = []
    for k in group:
        piece = lambda start, count: sum(row_piece(corr, k, start, count) for corr in corrs)
        a = (
            tabs["ends_x"][...]
            + jnp.where(row == 2, piece(2 * ny, nx), 0.0)
            + jnp.where(row == 3, piece(2 * ny + nx, nx), 0.0)
        )
        b = (
            tabs["ends_y"][...]
            + jnp.where(row == 0, piece(0, ny), 0.0)
            + jnp.where(row == 1, piece(ny, ny), 0.0)
        )
        spectra.append(spec[k] + tabs["inverse"][...] * outer_sum(a, b))
    lines = times_left(tabs["inv_x"], jnp.concatenate(spectra, axis=1))
    lines = jnp.concatenate([lines[:, i * ly : (i + 1) * ly] for i in range(len(group))], axis=0)
    fields = lines_back(lines, tabs)
    return [fields[i * lx : (i + 1) * lx] for i in range(len(group))]


def add_rim(field, k, rim_rows, rim_cols):
    kinds, lx, ly = field.shape
    field[k, 0:1, :] += rim_rows[k : k + 1, :]
    field[k, lx - 1 : lx, :] += rim_rows[kinds + k : kinds + k + 1, :]
    row = lax.broadcasted_iota(jnp.int32, (8, 1), 0)
    at = lax.broadcasted_iota(jnp.int32, (8, 128), 1)
    for start, source, lane in ((0, k, 0), (ly - 128, kinds + k, 127)):
        cells = jnp.where(row == 0, rim_cols[source : source + 1, :], 0.0)
        where = jnp.where((row == 0) & (at == lane), 1.0, 0.0).astype(F32)
        field[k, :, start : start + 128] += outer_sum(cells, where)


def lane_sum(x):
    return jnp.sum(x, axis=0, keepdims=True)


def store_sums(pay, start, rows):
    rest = pay.shape[1] - start
    row = lax.broadcasted_iota(jnp.int32, (rest, 128), 0)
    block = jnp.zeros((rest, 128), F32)
    for j, value in enumerate(rows):
        block = jnp.where(row == j, value, block)
    for d in range(pay.shape[0]):
        pay[d, start:, :] = block


OUT = ("fwd_ye", "fwd_yo", "fwd_x", "inverse", "edge_x", "edge_y")
BACK = ("inv_ye", "inv_yo", "inv_x", "inverse", "ends_x", "ends_y")
MAIN = OUT + ("inv_ye", "inv_yo", "inv_x", "ends_x", "ends_y")
RIM = ("cross", "cross_t", "cos_xt", "self_x", "self_y")
GROUP = 2
FACE = (
    "cross",
    "cross_t",
    "cos_x",
    "cos_xt",
    "gap_x",
    "gap_y",
    "fourier",
    "twist",
    "gather",
    "scatter",
)


def destinations(k, kinds, gx, gy):
    return [k * gy + p + kinds * gy * copy for copy in range(gx // kinds) for p in range(gy)]


def store_line(pay, places, line):
    for d in places:
        for j in range(line.shape[1] // 128):
            pay[d, j : j + 1, :] = line[:, j * 128 : (j + 1) * 128]


def edge_kernel(_, state, rows_first, rows_last, cols_first, cols_last, tiles, sem):
    kinds, lx = cols_first.shape
    last = state.shape[3] - 128
    copies = [
        pltpu.make_async_copy(state.at[0, 0], rows_first, sem.at[0]),
        pltpu.make_async_copy(state.at[lx - 1, 0], rows_last, sem.at[1]),
    ]
    for k in range(kinds):
        for n, start in enumerate((0, last)):
            copies.append(
                pltpu.make_async_copy(
                    state.at[:, 0, k, pl.ds(start, 128)],
                    tiles.at[k, :, pl.ds(n * 128, 128)],
                    sem.at[2 + 2 * k + n],
                )
            )
    for copy in copies:
        copy.start()
    row = lax.broadcasted_iota(jnp.int32, (8, 256), 0)
    lane = lax.broadcasted_iota(jnp.int32, (8, 256), 1)
    pick = jnp.where(((row == 0) & (lane == 0)) | ((row == 1) & (lane == 255)), 1.0, 0.0)
    pick = jnp.concatenate([pick] * 3, axis=1).astype(BF16)
    for copy in copies[2:]:
        copy.wait()
    for k in range(kinds):
        cells = jnp.concatenate(thirds(tiles[k]), axis=1).astype(BF16)
        ends = lax.dot_general(pick, cells, (((1,), (1,)), ((), ())), preferred_element_type=F32)
        cols_first[k : k + 1, :] = ends[0:1]
        cols_last[k : k + 1, :] = ends[1:2]
    for copy in copies[:2]:
        copy.wait()


def start_kernel(parts, names, places, state, mob_hbm, *refs):
    packs, refs = refs[:2], refs[2:]
    count = len(names)
    tabs = dict(zip(names, refs[:count]))
    cells, mob, r0, spec, line_out = refs[count : count + 5]
    st, field, lines, base, sem, tab_sem = refs[count + 5 :]
    lx, kinds, ly = field.shape
    size = lx // parts
    copies = [
        pltpu.make_async_copy(state.at[pl.ds(c * size, size), 0], st.at[pl.ds(1 + c * size, size)], sem.at[c])
        for c in range(parts)
    ]
    mob_copy = pltpu.make_async_copy(mob_hbm.at[:, 0, :], mob, sem.at[parts])
    mob_copy.start()
    for copy in copies:
        copy.start()
    loads = {name: [] for name in names}
    for n, (name, which, start, rows, j, _) in enumerate(places):
        loads[name].append(
            pltpu.make_async_copy(
                packs[which].at[pl.ds(start, rows)], tabs[name].at[:, pl.ds(j * 128, 128)], tab_sem.at[n]
            )
        )
    for name in names:
        for copy in loads[name]:
            copy.start()
    lane = lax.broadcasted_iota(jnp.int32, (kinds, ly), 1)

    def force(start):
        for i in range(size // 8):
            row = pl.multiple_of(start + i * 8, 8)
            total = sum(st[pl.ds(row + 1, 8), k, :] ** 2 for k in range(kinds))
            base[i] = -linear_coef + 2.0 * cross_coef * total
            rates = time_step * mob[pl.ds(row, 8), :]
            for j in range(8):
                mid = st[row + 1 + j]
                left = jnp.where(lane == 0, mid, pltpu.roll(mid, 1, 1))
                right = jnp.where(lane == ly - 1, mid, pltpu.roll(mid, ly - 1, 1))
                lap = (st[row + j] + st[row + 2 + j]) + (left + right) - 4.0 * mid
                react = mid * (base[i, j : j + 1, :] + (cubic_coef - 2.0 * cross_coef) * (mid * mid))
                field[row + j] = rates[j : j + 1, :] * (gradient_coef * lap - react)

    def rows_out(start):
        rows = field[pl.ds(start, size)].reshape(size * kinds, ly)
        lines[pl.ds(start, size)] = lines_out(rows, tabs).reshape(size, kinds, ly)

    mob_copy.wait()
    copies[0].wait()
    copies[1].wait()
    st[0] = st[1]
    force(0)
    for copy in copies[2:]:
        copy.wait()
    st[lx + 1] = st[lx]
    for name in OUT:
        for copy in loads[name]:
            copy.wait()

    @pl.loop(1, parts)
    def _(c):
        rows_out(pl.multiple_of((c - 1) * size, size))
        force(pl.multiple_of(c * size, size))

    rows_out(lx - size)

    @pl.loop(0, lx // 8)
    def _(i):
        row = pl.multiple_of(i * 8, 8)
        for k in range(kinds):
            cells[k, pl.ds(row, 8), :] = st[pl.ds(row + 1, 8), k, :]
            r0[k, pl.ds(row, 8), :] = field[pl.ds(row, 8), k, :]

    for k in range(0, kinds, GROUP):
        group = list(range(k, k + GROUP))
        modes_out(
            [lines[:, g, :] for g in group], group, spec, tabs, lambda g, line: store_line(line_out, [g], line)
        )
    for name in names:
        for copy in loads[name]:
            if name not in OUT:
                copy.wait()


def rim_kernel(gx, gy, lx, ly, *refs):
    line, lo, hi, near_left, near_right, own_left, own_right, st, mob = refs[:9]
    names = RIM + ("fwd_ye", "fwd_yo")
    tabs = dict(zip(names, refs[9 : 9 + len(names)]))
    pay, corr, rows_out, cols_out = refs[9 + len(names) :]
    kinds = line.shape[0]
    nx, ny = lx // 128, ly // 128
    hx, hy = lx // 2, ly // 2
    dot = functools.partial(jnp.dot, precision=lax.Precision.HIGHEST, preferred_element_type=F32)

    def column(start, lane):
        where = jnp.where(lax.broadcasted_iota(jnp.int32, (8, 128), 1) == lane, 1.0, 0.0).astype(F32)
        return lax.dot_general(
            where,
            mob[:, start : start + 128],
            (((1,), (1,)), ((), ())),
            precision=lax.Precision.HIGHEST,
            preferred_element_type=F32,
        )

    top = stiffness * mob[0:1, :] * (lo[...] - st[:, 0, :])
    bottom = stiffness * mob[lx - 1 : lx, :] * (hi[...] - st[:, lx - 1, :])
    left = stiffness * column(0, 0) * (near_left[...] - own_left[...])
    right = stiffness * column(ly - 128, 127) * (near_right[...] - own_right[...])
    rows = jnp.concatenate([top, bottom], axis=0)
    cols = jnp.concatenate([left, right], axis=0)
    rows_out[...] = rows
    cols_out[...] = cols
    rows = lines_out(rows, tabs)
    cols = dot(cols, tabs["cos_xt"][...])
    row_even, row_odd = rows[:kinds] + rows[kinds:], rows[:kinds] - rows[kinds:]
    col_even, col_odd = cols[:kinds] + cols[kinds:], cols[:kinds] - cols[kinds:]

    def spread(even, odd, table, width):
        both = dot(jnp.concatenate([even, odd], axis=0), table)
        lane = lax.broadcasted_iota(jnp.int32, (kinds, both.shape[1]), 1)
        return jnp.where(lane < width, both[:kinds], both[kinds:])

    add = [
        tabs["self_x"][0:1, :] * row_even + spread(col_even[:, :hx], col_odd[:, :hx], tabs["cross"][:hx, :], hy),
        tabs["self_x"][1:2, :] * row_odd + spread(col_even[:, hx:], col_odd[:, hx:], tabs["cross"][hx:, :], hy),
        tabs["self_y"][0:1, :] * col_even
        + spread(row_even[:, :hy], row_odd[:, :hy], tabs["cross_t"][:hy, :], hx),
        tabs["self_y"][1:2, :] * col_odd
        + spread(row_even[:, hy:], row_odd[:, hy:], tabs["cross_t"][hy:, :], hx),
    ]
    add = jnp.concatenate(add, axis=1)
    share = jnp.concatenate([row_even, row_odd, col_even, col_odd], axis=1)
    count = 2 * (nx + ny)
    for j in range(corr.shape[1]):
        if j < count:
            corr[:, j, :] = share[:, j * 128 : (j + 1) * 128]
            value = line[:, j, :] + add[:, j * 128 : (j + 1) * 128]
        else:
            corr[:, j, :] = jnp.zeros((kinds, 128), F32)
            value = jnp.zeros((kinds, 128), F32)
        for copy in range(gx // kinds):
            for p in range(gy):
                pay[pl.ds(copy * kinds * gy + p, kinds, stride=gy), j, :] = value


def middle_kernel(gx, gy, nrow, *refs):
    corr, rim, rim_rows, rim_cols, st, mob, _, _ = refs[:8]
    tabs = dict(zip(MAIN, refs[8 : 8 + len(MAIN)]))
    r0, spec, field, q1, pay, acc = refs[8 + len(MAIN) :]
    kinds, lx, ly = r0.shape
    acc[...] = jnp.zeros_like(acc)
    for k in range(0, kinds, GROUP):
        group = list(range(k, k + GROUP))
        for g, cells in zip(group, transform_back(spec, group, (corr, rim), tabs)):
            field[g] = cells
            add_rim(r0, g, rim_rows, rim_cols)

    @pl.loop(0, lx // 8)
    def _(i):
        row = pl.multiple_of(i * 8, 8)
        for j in range(ly // 128):
            lanes = slice(j * 128, (j + 1) * 128)
            move = mob[pl.ds(row, 8), lanes]
            rate = time_step * move
            s = [st[k, pl.ds(row, 8), lanes] for k in range(kinds)]
            z = [field[k, pl.ds(row, 8), lanes] for k in range(kinds)]
            squares = [v * v for v in s]
            total = sum(squares)
            coupled = sum(a * b for a, b in zip(s, z))
            base = 1.0 - move + rate * (-linear_coef + 2.0 * cross_coef * total)
            square_coef = (3.0 * cubic_coef - 6.0 * cross_coef) * rate
            pull = (4.0 * cross_coef) * rate * coupled
            parts = [jnp.zeros((8, 128), F32)] * 2
            for k in range(kinds):
                old = r0[k, pl.ds(row, 8), lanes]
                image = z[k] * (base + square_coef * squares[k]) + pull * s[k] + move * old
                q1[k, pl.ds(row, 8), lanes] = image
                pairs = ((old, old), (old, image))
                parts = [p + a * b for p, (a, b) in zip(parts, pairs)]
            for n in range(2):
                acc[n] += parts[n]

    for k in range(0, kinds, GROUP):
        group = list(range(k, k + GROUP))
        lines = lines_out(jnp.concatenate([q1[g] for g in group], axis=0), tabs)
        modes_out(
            [lines[i * lx : (i + 1) * lx] for i in range(GROUP)],
            group,
            spec,
            tabs,
            lambda g, line: store_line(pay, destinations(g, kinds, gx, gy), line),
        )
    store_sums(pay, nrow, [lane_sum(acc[n]) for n in range(2)])


def last_kernel(nrow, *refs):
    corr, st, mob, spec, r0, q1, z1 = refs[:7]
    tabs = dict(zip(BACK, refs[7 : 7 + len(BACK)]))
    field, sums, acc = refs[7 + len(BACK) :]
    kinds, lx, ly = r0.shape
    acc[...] = jnp.zeros_like(acc)
    height = corr[0, nrow + 1 : nrow + 2, :] / corr[0, nrow : nrow + 1, :]
    for k in range(0, kinds, GROUP):
        group = list(range(k, k + GROUP))
        for g, cells in zip(group, transform_back(spec, group, (corr,), tabs)):
            field[g] = cells - height[:, :1] * z1[g]

    @pl.loop(0, lx // 8)
    def _(i):
        row = pl.multiple_of(i * 8, 8)
        for j in range(ly // 128):
            lanes = slice(j * 128, (j + 1) * 128)
            move = mob[pl.ds(row, 8), lanes]
            rate = time_step * move
            s = [st[k, pl.ds(row, 8), lanes] for k in range(kinds)]
            z = [field[k, pl.ds(row, 8), lanes] for k in range(kinds)]
            squares = [v * v for v in s]
            total = sum(squares)
            coupled = sum(a * b for a, b in zip(s, z))
            base = 1.0 - move + rate * (-linear_coef + 2.0 * cross_coef * total)
            square_coef = (3.0 * cubic_coef - 6.0 * cross_coef) * rate
            pull = (4.0 * cross_coef) * rate * coupled
            parts = [jnp.zeros((8, 128), F32)] * 4
            for k in range(kinds):
                old = r0[k, pl.ds(row, 8), lanes]
                basis = q1[k, pl.ds(row, 8), lanes] - height * old
                image = z[k] * (base + square_coef * squares[k]) + pull * s[k] + move * basis
                pairs = ((basis, basis), (basis, image), (old, image), (image, image))
                parts = [p + a * b for p, (a, b) in zip(parts, pairs)]
            for n in range(4):
                acc[n] += parts[n]

    store_sums(sums, 0, [lane_sum(acc[n]) for n in range(4)])


def face_kernel(gx, gy, lx, ly, nrow, place, pay, *refs):
    tabs = dict(zip(FACE, refs))
    out = refs[len(FACE)]
    nx, ny = lx // 128, ly // 128
    hx, hy = lx // 2, ly // 2
    blocks = gx * gy
    dot = functools.partial(jnp.dot, precision=lax.Precision.HIGHEST, preferred_element_type=F32)
    piece = lambda start, count: jnp.concatenate([pay[:, start + j, :] for j in range(count)], axis=1)
    t_even, t_odd = piece(0, ny), piece(ny, ny)
    s_even, s_odd = piece(2 * ny, nx), piece(2 * ny + nx, nx)

    def turn(a, shift):
        shift = shift % a.shape[0]
        return a if shift == 0 else pltpu.roll(a, shift, 0)

    def group(a, shift):
        by = lax.broadcasted_iota(jnp.int32, a.shape, 0) % gy
        shift = shift % gy
        if shift == 0:
            return a
        return jnp.where(by < gy - shift, turn(a, -shift), turn(a, gy - shift))

    def circulant(coef, a, move, count):
        value = coef(0) * a
        for d in range(1, count // 2 + 1):
            near = move(a, d) if 2 * d == count else move(a, d) + move(a, -d)
            value = value + coef(d) * near
        return value

    def solve_x(jump, step):
        return circulant(lambda d: tabs["gap_x"][d : d + 1, :], jump, lambda a, d: turn(a, -d * step), gx)

    def spread(minus, plus, table, width):
        count = minus.shape[0]
        both = dot(jnp.concatenate([minus, plus], axis=0), table)
        lane = lax.broadcasted_iota(jnp.int32, (count, both.shape[1]), 1)
        return jnp.where(lane < width, -both[:count], both[count:])

    flux = solve_x(t_even - t_odd - turn(t_even + t_odd, -gy), gy)
    minus, plus = flux - turn(flux, gy), flux + turn(flux, gy)
    s_even = s_even + spread(minus[:, :hy], plus[:, :hy], tabs["cross_t"][:hy, :], hx)
    s_odd = s_odd + spread(minus[:, hy:], plus[:, hy:], tabs["cross_t"][hy:, :], hx)
    jump = s_even - s_odd - group(s_even + s_odd, 1)
    lines = dot(tabs["gather"][:, :blocks], dot(jump, tabs["cos_x"][...]))
    rows = lines.shape[0] // 2
    real, imag = lines[:rows], lines[rows:]
    cosine, sine = tabs["twist"][:rows, :], tabs["twist"][rows:, :]
    turned = jnp.concatenate([real * cosine + imag * sine, imag * cosine - real * sine], axis=0)
    both = dot(turned, tabs["fourier"][...])
    waves = jnp.concatenate(
        [both[:rows, :lx] + both[rows:, lx:], both[rows:, :lx] - both[:rows, lx:]], axis=0
    )
    waves = circulant(lambda d: tabs["gap_y"][2 * rows * d : 2 * rows * (d + 1), :], waves, group, gy)
    both = dot(waves, tabs["fourier"][...])
    real = both[:rows, :lx] - both[rows:, lx:]
    imag = both[:rows, lx:] + both[rows:, :lx]
    turned = jnp.concatenate([real * cosine - imag * sine, real * sine + imag * cosine], axis=0)
    flow = dot(dot(tabs["scatter"][:, : 2 * rows], turned), tabs["cos_xt"][...])
    flow_minus, flow_plus = flow - group(flow, -1), flow + group(flow, -1)
    row = lax.broadcasted_iota(jnp.int32, (gx, blocks), 0)
    col = lax.broadcasted_iota(jnp.int32, (gx, blocks), 1)
    pick = jnp.where(col == row * gy + place[0], 1.0, 0.0).astype(F32)
    chosen = dot(pick, jnp.concatenate([t_even, t_odd, flow_minus, flow_plus], axis=1))
    t_even, t_odd = chosen[:, :ly], chosen[:, ly : 2 * ly]
    minus, plus = chosen[:, 2 * ly : 2 * ly + lx], chosen[:, 2 * ly + lx :]
    t_even = t_even + spread(minus[:, :hx], plus[:, :hx], tabs["cross"][:hx, :], hy)
    t_odd = t_odd + spread(minus[:, hx:], plus[:, hx:], tabs["cross"][hx:, :], hy)
    flux = solve_x(t_even - t_odd - turn(t_even + t_odd, -1), 1)
    line = jnp.concatenate([turn(flux, 1) - flux, flux + turn(flux, 1), -minus, plus], axis=1)
    for j in range(line.shape[1] // 128):
        out[:, j, :] = line[:, j * 128 : (j + 1) * 128]
    for n in range(nrow, nrow + 2):
        total = jnp.sum(jnp.sum(pay[:, n, :], axis=0, keepdims=True), axis=1, keepdims=True)
        out[:, n, :] = jnp.broadcast_to(total, (gx, 128))


def finish_kernel(nrow, sums, corr, st, z1, z2, out_hbm, out, sem):
    beta_sq = corr[0, nrow : nrow + 1, :]
    top_left = corr[0, nrow + 1 : nrow + 2, :] / beta_sq
    beta = jnp.sqrt(beta_sq)
    total = jnp.sum(jnp.sum(sums[...], axis=0), axis=1, keepdims=True)
    total = jnp.broadcast_to(total, (8, 128))
    length_sq, cross, first, image_sq = [total[n : n + 1, :] for n in range(4)]
    length = jnp.sqrt(length_sq)
    below_first = length / beta
    top_right = first / (beta * length)
    middle_right = cross / length_sq
    bottom_sq = image_sq / length_sq - top_right * top_right - middle_right * middle_right
    first_radius = jnp.sqrt(top_left * top_left + below_first * below_first)
    first_cosine = top_left / first_radius
    first_sine = below_first / first_radius
    upper_right = first_cosine * top_right + first_sine * middle_right
    lower_right = -first_sine * top_right + first_cosine * middle_right
    lower_target = -first_sine * beta
    second_coef = lower_right * lower_target / (lower_right * lower_right + jnp.maximum(bottom_sq, 0.0))
    first_coef = (first_cosine * beta - upper_right * second_coef) / first_radius
    a = (first_coef / beta)[:, :1]
    b = (second_coef / length)[:, :1]
    lx, kinds, ly = out.shape
    parts = sem.shape[0]
    size = lx // parts
    copies = []
    for c in range(parts):

        @pl.loop(c * size // 8, (c + 1) * size // 8)
        def _(i):
            row = pl.multiple_of(i * 8, 8)
            for k in range(kinds):
                update = a * z1[k, pl.ds(row, 8), :] + b * z2[k, pl.ds(row, 8), :]
                out[pl.ds(row, 8), k, :] = st[k, pl.ds(row, 8), :] + update

        copies.append(
            pltpu.make_async_copy(
                out.at[pl.ds(c * size, size)], out_hbm.at[pl.ds(c * size, size), 0], sem.at[c]
            )
        )
        copies[-1].start()
    for copy in copies:
        copy.wait()


def halo(rows_first, rows_last, cols_first, cols_last):
    def shift(cells, axis, step):
        count = lax.axis_size(axis)
        return lax.ppermute(cells, axis, [(i, (i + step) % count) for i in range(count)])

    return (
        shift(rows_last, "gx", 1),
        shift(rows_first, "gx", -1),
        shift(cols_last, "gy", 1),
        shift(cols_first, "gy", -1),
    )


def body(gx, gy, state, mobility):
    lx, _, kinds, ly = state.shape
    main, face = make_tables(lx, ly, gx, gy)
    tables = {**main, **face}
    names = list(OUT) + [name for name in tables if name not in OUT]
    packs, places = packed(tables)
    pick = lambda some: [tables[name] for name in some]
    rest = lambda some: [tables[name] for name in names if name not in some]
    nrow = (2 * lx + 2 * ly) // 128
    width = -(-(nrow + 2) // 8) * 8
    vmem = pl.BlockSpec(memory_space=pltpu.VMEM)
    hbm = pl.BlockSpec(memory_space=pl.ANY)
    smem = pl.BlockSpec(memory_space=pltpu.SMEM)
    grant = lambda mib: pltpu.CompilerParams(vmem_limit_bytes=mib * 1024 * 1024)
    array = lambda *shape: jax.ShapeDtypeStruct(shape, F32)
    whole = array(kinds, lx, ly)
    payload = array(gx * gy, width, 128)
    dma = pltpu.SemaphoreType.DMA
    place = lax.axis_index("gy").astype(jnp.int32).reshape(1)

    def kernel(function, name, inputs, keep, **options):
        count = len(inputs)

        def run(*refs):
            function(*refs[:count], *refs[count + len(keep) :])

        specs = [smem if x is place else vmem for x in inputs] + [vmem] * len(keep)
        return pl.pallas_call(
            run, in_specs=specs, compiler_params=grant(GRANTS[name]), name=name, **options
        )(*inputs, *keep)

    def faces(pay, keep):
        pay = lax.all_to_all(pay, ("gx", "gy"), split_axis=0, concat_axis=0, tiled=True)
        fluxes = kernel(
            functools.partial(face_kernel, gx, gy, lx, ly, nrow),
            "faces",
            [place, pay, *pick(FACE)],
            keep + rest(FACE),
            out_shape=array(gx, width, 128),
            out_specs=vmem,
        )
        return lax.all_to_all(fluxes, "gx", split_axis=0, concat_axis=0, tiled=True)

    rows, cols = array(kinds, ly), array(kinds, lx)
    edges = pl.pallas_call(
        edge_kernel,
        out_shape=(rows, rows, cols, cols),
        in_specs=[smem, hbm],
        out_specs=(vmem,) * 4,
        scratch_shapes=[pltpu.VMEM((kinds, lx, 256), F32), dma((2 + 2 * kinds,))],
        compiler_params=grant(GRANTS["edges"]),
        name="edges",
    )(place, state)
    near = halo(*edges)
    parts = 4
    wide = {name: (count, width) for name, _, _, count, _, width in places}
    shapes = [jax.ShapeDtypeStruct(wide[name], tables[name].dtype) for name in names]
    outs = pl.pallas_call(
        functools.partial(start_kernel, parts, names, places),
        out_shape=(*shapes, whole, array(lx, ly), whole, whole, array(kinds, width, 128)),
        in_specs=[hbm] * 4,
        out_specs=(vmem,) * (5 + len(names)),
        scratch_shapes=[
            pltpu.VMEM((lx + 2, kinds, ly), F32),
            pltpu.VMEM((lx, kinds, ly), F32),
            pltpu.VMEM((lx, kinds, ly), F32),
            pltpu.VMEM((lx // parts // 8, 8, ly), F32),
            dma((parts + 1,)),
            dma((len(places),)),
        ],
        compiler_params=grant(GRANTS["start"]),
        cost_estimate=pl.CostEstimate(flops=10**10, bytes_accessed=2 * 10**7, transcendentals=0),
        name="start",
    )(state, mobility, *[jnp.asarray(pack) for pack in packs])
    tables = dict(zip(names, outs))
    st, mob, r0, spec, line = outs[len(names) :]
    some = RIM + ("fwd_ye", "fwd_yo")
    pay, rim, rim_rows, rim_cols = kernel(
        functools.partial(rim_kernel, gx, gy, lx, ly),
        "rim",
        [line, *near, *edges[2:], st, mob, *pick(some)],
        [r0, spec] + rest(some),
        out_shape=(payload, array(kinds, width, 128), array(2 * kinds, ly), array(2 * kinds, lx)),
        out_specs=(vmem,) * 4,
    )
    corr = faces(pay, [st, mob, r0, spec, rim, rim_rows, rim_cols])
    r0, spec, z1, q1, pay = kernel(
        functools.partial(middle_kernel, gx, gy, nrow),
        "middle",
        [corr, rim, rim_rows, rim_cols, st, mob, r0, spec, *pick(MAIN)],
        rest(MAIN),
        out_shape=(whole, whole, whole, whole, payload),
        out_specs=(vmem,) * 5,
        scratch_shapes=[pltpu.VMEM((2, 8, 128), F32)],
        input_output_aliases={6: 0, 7: 1},
    )
    corr = faces(pay, [st, mob, r0, spec, z1, q1])
    z2, sums = kernel(
        functools.partial(last_kernel, nrow),
        "last",
        [corr, st, mob, spec, r0, q1, z1, *pick(BACK)],
        [],
        out_shape=(whole, array(gx * gy, 8, 128)),
        out_specs=(vmem,) * 2,
        scratch_shapes=[pltpu.VMEM((4, 8, 128), F32)],
    )
    sums = lax.all_to_all(sums, ("gx", "gy"), split_axis=0, concat_axis=0, tiled=True)
    return kernel(
        functools.partial(finish_kernel, nrow),
        "finish",
        [sums, corr, st, z1, z2],
        [],
        out_shape=jax.ShapeDtypeStruct(state.shape, F32),
        out_specs=hbm,
        scratch_shapes=[pltpu.VMEM((lx, kinds, ly), F32), dma((4,))],
    )


def solution(mesh):
    return jax.shard_map(
        functools.partial(body, mesh.shape["gx"], mesh.shape["gy"]),
        mesh=mesh,
        in_specs=(P("gx", None, None, "gy"), P("gx", None, "gy")),
        out_specs=P("gx", None, None, "gy"),
        check_vma=False,
    )
```

time: 167 us -> 116 us (0.69)
  Pallas kernels: 87.6 us -> 48.2 us
  waiting for transfers between devices: 15.7 us -> 0.01 us
  blocking collectives: 47.1 us -> 54.8 us
  starting transfers between devices: 9.6 us -> 7.81 us
    pallas_call x6 -> x8, Pallas kernels: 87.6 us -> 48.2 us  [the longest x6 31.8 us: kernel(): pl.pallas_call(run, in_specs=specs, compiler_params=grant(GRANTS[name]),...]
    all_to_all x1 -> x2, blocking collectives: 13.9 us -> 26 us  [faces(): lax.all_to_all(pay, ('gx', 'gy'), split_axis=0, concat_axis=0, tiled=True)]
    all_to_all x1 -> x0, waiting for transfers between devices: 10.6 us -> none  [faces(): lax.all_to_all(pay, ('gx', 'gy'), split_axis=0, concat_axis=0, tiled=True)]
    ppermute x4, waiting for transfers between devices: 5.1 us -> 0.01 us  [shift(): lax.ppermute(cells, axis, [(i, (i + step) % count) for i in range(count)])]
    all_to_all x2, blocking collectives: 21.7 us -> 18.9 us  [faces(): return lax.all_to_all(fluxes, 'gx', split_axis=0, concat_axis=0, tiled=True)]
    slice x2 -> x0, local copies, waits for them, and re-layouts: 2.63 us -> none  [the longest x1 1.89 us: halo(): left = shift(column(state[..., -1:]), 'gy', 1)]
    all_to_all x1 -> x0, starting transfers between devices: 2.6 us -> none  [faces(): lax.all_to_all(pay, ('gx', 'gy'), split_axis=0, concat_axis=0, tiled=True)]
    unnamed x8 -> x12, local copies, waits for them, and re-layouts: 2.06 us -> 4.59 us
  transfers between devices with their start and end apart: 5 -> 4, of which waited for: 3 -> 0; matrix products, arithmetic and copies ran while one was open for 1% -> 0% of each run, Pallas kernels for 0% -> 11%
where the time goes in v2:
time: 116 us
  blocking collectives  54.8 us (47%)
  Pallas kernels  48.2 us (42%)
  starting transfers between devices  7.81 us (7%)
  local copies, waits for them, and re-layouts  4.59 us (4%)
    pallas_call x6, Pallas kernels, kernel(): pl.pallas_call(run, in_specs=specs, compiler_params=grant(GRANTS[name]),...  31.8 us
    all_to_all x2, blocking collectives, faces(): lax.all_to_all(pay, ('gx', 'gy'), split_axis=0, concat_axis=0, tiled=True)  26 us
    all_to_all x2, blocking collectives, faces(): return lax.all_to_all(fluxes, 'gx', split_axis=0, concat_axis=0, tiled=True)  18.9 us
    pallas_call x1, Pallas kernels, body(): pl.pallas_call(functools.partial(start_kernel, parts, names, places), out...  12.6 us
    all_to_all x1, blocking collectives, body(): lax.all_to_all(sums, ('gx', 'gy'), split_axis=0, concat_axis=0, tiled=True)  9.93 us
    ppermute x4, starting transfers between devices, shift(): lax.ppermute(cells, axis, [(i, (i + step) % count) for i in range(count)])  7.81 us
    unnamed x12, local copies, waits for them, and re-layouts  4.59 us
    pallas_call x1, Pallas kernels, body(): pl.pallas_call(edge_kernel, out_shape=(rows, rows, cols, cols), in_specs=...  3.76 us
  transfers between devices with their start and end apart: 4, of which 0 were waited for; matrix products, arithmetic and copies ran while one was open for 0% of the time, Pallas kernels for 11%

profile of v2, /device:TPU:0, one launch (start us, length us, event | category | flops | bytes accessed | tf_op | source)
XLA Modules:
  0.0 115.7 jit_solution(9588020721566261770)
XLA Ops:
  0.0 0.0 copy-start
  0.0 3.8 %edges.1 = (f32[8,512]{1,0:T(8,128)}, f32[8,512]{1,0:T(8,128)}, f32[8,256]{1,0:T(8,128)}, f32[8,256]{1,0:T(8,128)}) custom-call(s32[1]{0:T(128)} %bitcast._.refs_0_, f32[256,1,8,512]{3,2,1,0:T(8,128)} %state.3), custom_call_target="tpu_custom_call" | custom-call | tf_op jit(solution)/shard_map/edges/pallas_call | solution.py:765
  3.8 0.5 collective-permute-start.2
  4.3 2.0 %collective-permute-start.3 = (f32[8,256]{1,0:T(8,128)}, f32[8,256]{1,0:T(8,128)S(1)}, u32[]{:S(2)}, u32[]{:S(2)}) collective-permute-start(f32[8,256]{1,0:T(8,128)} %get-tuple-element.52.refs_5_), channel_id=1, source_target_pairs={{0,3},{1,0},{2,1},{3,2},{4,7},{5,4},{6,5},{7,6},{8,11},{9,8},{10,9... | collective-permute-start | bytes 24584 | tf_op jit(solution)/shard_map/ppermute | solution.py:711
  6.3 2.3 %collective-permute-start = (f32[8,512]{1,0:T(8,128)}, f32[8,512]{1,0:T(8,128)S(1)}, u32[]{:S(2)}, u32[]{:S(2)}) collective-permute-start(f32[8,512]{1,0:T(8,128)} %get-tuple-element.49), channel_id=1, source_target_pairs={{0,4},{4,8},{8,12},{12,16},{16,20},{20,24},{24,28},{28,0},{1,5},{5... | collective-permute-start | bytes 49160 | tf_op jit(solution)/shard_map/ppermute | solution.py:711
  8.5 0.0 copy-start.1
  8.5 0.0 copy-start.2
  8.5 3.0 %collective-permute-start.1 = (f32[8,512]{1,0:T(8,128)}, f32[8,512]{1,0:T(8,128)S(1)}, u32[]{:S(2)}, u32[]{:S(2)}) collective-permute-start(f32[8,512]{1,0:T(8,128)} %get-tuple-element.50), channel_id=1, source_target_pairs={{0,28},{4,0},{8,4},{12,8},{16,12},{20,16},{24,20},{28,24},{1,29},{... | collective-permute-start | bytes 49160 | tf_op jit(solution)/shard_map/ppermute | solution.py:711
  11.6 0.0 copy-done
  11.6 0.0 copy-start.3
  11.6 1.0 copy-done.3
  12.6 0.0 copy-start.4
  12.6 1.9 %copy-done.4 = f32[6000,128]{1,0:T(8,128)S(1)} copy-done((f32[6000,128]{1,0:T(8,128)S(1)}, f32[6000,128]{1,0:T(8,128)}, u32[]{:S(2)}) %copy-start.4) | copy-done | bytes 3072024
  14.5 1.7 %copy-done.5 = bf16[9216,128]{1,0:T(8,128)(2,1)S(1)} copy-done((bf16[9216,128]{1,0:T(8,128)(2,1)S(1)}, bf16[9216,128]{1,0:T(8,128)(2,1)}, u32[]{:S(2)}) %copy-start.5) | copy-done | bytes 2359320
  16.2 12.6 %start.1 = (bf16[768,256]{1,0:T(8,128)(2,1)S(1)}, bf16[768,256]{1,0:T(8,128)(2,1)S(1)}, bf16[256,768]{1,0:T(8,128)(2,1)S(1)}, f32[256,512]{1,0:T(8,128)S(1)}, f3...) custom-call(f32[256,1,8,512]{3,2,1,0:T(8,128)S(1)} %copy-done, ...), custom_call_target="tpu_custom_call" | custom-call | flops 10000000000 | bytes 20000000 | tf_op jit(solution)/shard_map/start/pallas_call | solution.py:778
  28.8 0.0 collective-permute-done.2.refs_3_
  28.8 0.0 collective-permute-done.3.refs_4_
  28.8 0.0 collective-permute-done.refs_1_
  28.8 0.0 collective-permute-done.1.refs_2_
  28.8 0.0 copy-done.1
  28.8 0.0 copy-done.2
  28.8 1.4 %rim.1 = (f32[32,16,128]{2,1,0:T(8,128)S(1)}, f32[8,16,128]{2,1,0:T(8,128)S(1)}, f32[16,512]{1,0:T(8,128)S(1)}, f32[16,256]{1,0:T(8,128)S(1)}) custom-call(f32[8,16,128]{2,1,0:T(8,128)S(1)} %get-tuple-element.48.refs_0_, f32[8,512]{1,0:T(8,128)S(1)} %collective-permute-done.refs_1_, f32[8,512]{1,0:T(8,128)S(1)} %collective-permute-done.1.refs_2_, ...), custom_call_target="tpu_custom_call" | custom-call | tf_op jit(solution)/shard_map/rim/pallas_call | solution.py:748
  30.2 13.7 %all_to_all.25.refs_1_ = f32[32,16,128]{2,1,0:T(8,128)S(1)} all-to-all(f32[32,16,128]{2,1,0:T(8,128)S(1)} %get-tuple-element.80), channel_id=1, replica_groups=mesh['gx'=8,'gy'=4] {'gx','gy'}, dimensions={0} | all-to-all | bytes 524288 | tf_op jit(solution)/shard_map/all_to_all | solution.py:753
  43.9 3.1 %faces.2 = f32[8,16,128]{2,1,0:T(8,128)S(1)} custom-call(s32[1]{0:T(128)} %bitcast._.refs_0_, f32[32,16,128]{2,1,0:T(8,128)S(1)} %all_to_all.25.refs_1_, f32[256,512]{1,0:T(8,128)S(1)} %get-tuple-element.55.refs_9_.refs_2_.refs_19_, f32[512,256]{1,0:T(8,128)S(1)} %get-tuple-element.56.refs_10_.refs_3_.refs_20_, ...), custom_call_target="tpu_custom_call" | custom-call | tf_op jit(solution)/shard_map/faces/pallas_call | solution.py:748
  47.0 9.5 %all_to_all.26.refs_0_ = f32[8,16,128]{2,1,0:T(8,128)S(1)} all-to-all(f32[8,16,128]{2,1,0:T(8,128)S(1)} %faces.2), channel_id=1, replica_groups=mesh['gx'=8,'gy'=4] {'gx'}, dimensions={0} | all-to-all | bytes 131072 | tf_op jit(solution)/shard_map/all_to_all | solution.py:762
  56.5 12.8 %middle.1 = (f32[8,256,512]{2,1,0:T(8,128)S(1)}, f32[8,256,512]{2,1,0:T(8,128)S(1)}, f32[8,256,512]{2,1,0:T(8,128)S(1)}, f32[8,256,512]{2,1,0:T(8,128)S(1)}, f32[32,16,128]{2,1,0:T(8,128)S(1)}) custom-call(f32[8,16,128]{2,1,0:T(8,128)S(1)} %all_to_all.26.refs_0_, ...), custom_call_target="tpu_custom_call", output_to_operand_aliasing={{0}: (6, {}), {1}: (7, {})} | custom-call | tf_op jit(solution)/shard_map/middle/pallas_call | solution.py:748
  69.3 12.3 %all_to_all.27.refs_1_ = f32[32,16,128]{2,1,0:T(8,128)S(1)} all-to-all(f32[32,16,128]{2,1,0:T(8,128)S(1)} %get-tuple-element.84), channel_id=1, replica_groups=mesh['gx'=8,'gy'=4] {'gx','gy'}, dimensions={0} | all-to-all | bytes 524288 | tf_op jit(solution)/shard_map/all_to_all | solution.py:753
  81.6 3.1 %faces.3 = f32[8,16,128]{2,1,0:T(8,128)S(1)} custom-call(s32[1]{0:T(128)} %bitcast._.refs_0_, f32[32,16,128]{2,1,0:T(8,128)S(1)} %all_to_all.27.refs_1_, f32[256,512]{1,0:T(8,128)S(1)} %get-tuple-element.55.refs_9_.refs_2_.refs_19_, f32[512,256]{1,0:T(8,128)S(1)} %get-tuple-element.56.refs_10_.refs_3_.refs_20_, ...), custom_call_target="tpu_custom_call" | custom-call | tf_op jit(solution)/shard_map/faces/pallas_call | solution.py:748
  84.7 9.4 %all_to_all.28.refs_0_.refs_1_ = f32[8,16,128]{2,1,0:T(8,128)S(1)} all-to-all(f32[8,16,128]{2,1,0:T(8,128)S(1)} %faces.3), channel_id=1, replica_groups=mesh['gx'=8,'gy'=4] {'gx'}, dimensions={0} | all-to-all | bytes 131072 | tf_op jit(solution)/shard_map/all_to_all | solution.py:762
  94.1 8.4 %last.1 = (f32[8,256,512]{2,1,0:T(8,128)S(1)}, f32[32,8,128]{2,1,0:T(8,128)S(1)}) custom-call(f32[8,16,128]{2,1,0:T(8,128)S(1)} %all_to_all.28.refs_0_.refs_1_, f32[8,256,512]{2,1,0:T(8,128)S(1)} %get-tuple-element.53.refs_7_.refs_12_.refs_4_.refs_1_.refs_2_, f32[256,512]{1,0:T(8,128)S(1)} %get-tuple-element.54.refs_8_.refs_13_.refs_5_.refs_2_, ...), custom_call_target="tpu_custom_call" | custom-call | tf_op jit(solution)/shard_map/last/pallas_call | solution.py:748
  102.4 9.9 %all_to_all.29.refs_0_ = f32[32,8,128]{2,1,0:T(8,128)S(1)} all-to-all(f32[32,8,128]{2,1,0:T(8,128)S(1)} %get-tuple-element.89), channel_id=1, replica_groups=mesh['gx'=8,'gy'=4] {'gx','gy'}, dimensions={0} | all-to-all | bytes 262144 | tf_op jit(solution)/shard_map/all_to_all | solution.py:827
  112.4 3.1 %finish.1 = f32[256,1,8,512]{3,2,1,0:T(8,128)} custom-call(f32[32,8,128]{2,1,0:T(8,128)S(1)} %all_to_all.29.refs_0_, f32[8,16,128]{2,1,0:T(8,128)S(1)} %all_to_all.28.refs_0_.refs_1_, f32[8,256,512]{2,1,0:T(8,128)S(1)} %get-tuple-element.53.refs_7_.refs_12_.refs_4_.refs_1_.refs_2_, f32[8,256,512]{2,1,0:T(8,128)S(1)} %get-tuple-element.87.refs_16_.refs_6_.refs_3_, ...), custom_call_target="tpu_custom_call" | custom-call | tf_op jit(solution)/shard_map/finish/pallas_call | solution.py:748
  (1 shorter events, 0.0 us)
Async XLA Ops:
  0.0 11.6 %copy-start = (f32[256,1,8,512]{3,2,1,0:T(8,128)S(1)}, f32[256,1,8,512]{3,2,1,0:T(8,128)}, u32[]{:S(2)}) copy-start(f32[256,1,8,512]{3,2,1,0:T(8,128)} %state.3) | copy-start | bytes 12582916
  3.8 25.0 %collective-permute-start.2 = (f32[8,256]{1,0:T(8,128)}, f32[8,256]{1,0:T(8,128)S(1)}, u32[]{:S(2)}, u32[]{:S(2)}) collective-permute-start(f32[8,256]{1,0:T(8,128)} %get-tuple-element.51.refs_6_), channel_id=1, source_target_pairs={{0,1},{1,2},{2,3},{3,0},{4,5},{5,6},{6,7},{7,4},{8,9},{9,10},{10,1... | collective-permute-start | bytes 24584 | tf_op jit(solution)/shard_map/ppermute | solution.py:711
  4.3 24.5 %collective-permute-start.3 = (f32[8,256]{1,0:T(8,128)}, f32[8,256]{1,0:T(8,128)S(1)}, u32[]{:S(2)}, u32[]{:S(2)}) collective-permute-start(f32[8,256]{1,0:T(8,128)} %get-tuple-element.52.refs_5_), channel_id=1, source_target_pairs={{0,3},{1,0},{2,1},{3,2},{4,7},{5,4},{6,5},{7,6},{8,11},{9,8},{10,9... | collective-permute-start | bytes 24584 | tf_op jit(solution)/shard_map/ppermute | solution.py:711
  6.3 22.5 %collective-permute-start = (f32[8,512]{1,0:T(8,128)}, f32[8,512]{1,0:T(8,128)S(1)}, u32[]{:S(2)}, u32[]{:S(2)}) collective-permute-start(f32[8,512]{1,0:T(8,128)} %get-tuple-element.49), channel_id=1, source_target_pairs={{0,4},{4,8},{8,12},{12,16},{16,20},{20,24},{24,28},{28,0},{1,5},{5... | collective-permute-start | bytes 49160 | tf_op jit(solution)/shard_map/ppermute | solution.py:711
  8.5 20.3 %copy-start.1 = (f32[8,256]{1,0:T(8,128)S(1)}, f32[8,256]{1,0:T(8,128)}, u32[]{:S(2)}) copy-start(f32[8,256]{1,0:T(8,128)} %get-tuple-element.52.refs_5_) | copy-start | bytes 24580
  8.5 20.3 %copy-start.2 = (f32[8,256]{1,0:T(8,128)S(1)}, f32[8,256]{1,0:T(8,128)}, u32[]{:S(2)}) copy-start(f32[8,256]{1,0:T(8,128)} %get-tuple-element.51.refs_6_) | copy-start | bytes 24580
  8.5 20.2 %collective-permute-start.1 = (f32[8,512]{1,0:T(8,128)}, f32[8,512]{1,0:T(8,128)S(1)}, u32[]{:S(2)}, u32[]{:S(2)}) collective-permute-start(f32[8,512]{1,0:T(8,128)} %get-tuple-element.50), channel_id=1, source_target_pairs={{0,28},{4,0},{8,4},{12,8},{16,12},{20,16},{24,20},{28,24},{1,29},{... | collective-permute-start | bytes 49160 | tf_op jit(solution)/shard_map/ppermute | solution.py:711
  11.6 1.0 copy-start.3
  12.6 1.9 %copy-start.4 = (f32[6000,128]{1,0:T(8,128)S(1)}, f32[6000,128]{1,0:T(8,128)}, u32[]{:S(2)}) copy-start(f32[6000,128]{1,0:T(8,128)} %constant.8.clone.refs_0_) | copy-start | bytes 9216004
  14.5 1.7 %copy-start.5 = (bf16[9216,128]{1,0:T(8,128)(2,1)S(1)}, bf16[9216,128]{1,0:T(8,128)(2,1)}, u32[]{:S(2)}) copy-start(bf16[9216,128]{1,0:T(8,128)(2,1)} %constant.9.clone.refs_1_) | copy-start | bytes 7077892

commit v3 on v2

--- a/solution.py
+++ b/solution.py
@@ -18,7 +18,7 @@
 
 F32 = jnp.float32
 BF16 = jnp.bfloat16
-GRANTS = dict(edges=56, start=20, rim=8, faces=8, middle=16, last=16, finish=8)
+GRANTS = dict(edges=4, start=13, rim=4, faces=4, middle=10, last=10, finish=6)
 
 
 def cosine_table(size):
@@ -96,17 +96,6 @@
                 scatter[i * gy + j, q * gy + j] = weight * np.cos(phase)
                 scatter[i * gy + j, rows + q * gy + j] = -weight * np.sin(phase)
     single = lambda a: np.ascontiguousarray(a, dtype=np.float32)
-    zero_x, zero_y = np.zeros(lx // 2), np.zeros(ly // 2)
-    ends_x = np.zeros((8, lx))
-    ends_x[0], ends_x[1] = (
-        np.concatenate([edge_x[: lx // 2], zero_x]),
-        np.concatenate([zero_x, edge_x[lx // 2 :]]),
-    )
-    ends_y = np.zeros((8, ly))
-    ends_y[2], ends_y[3] = (
-        np.concatenate([edge_y[: ly // 2], zero_y]),
-        np.concatenate([zero_y, edge_y[ly // 2 :]]),
-    )
     main = dict(
         fwd_ye=right_const(cos_y[: ly // 2, : ly // 2].T),
         fwd_yo=right_const(cos_y[ly // 2 :, : ly // 2].T),
@@ -117,42 +106,68 @@
         inverse=single(inverse),
         edge_x=single(np.repeat(edge_x[:, None], 128, axis=1)),
         edge_y=single(np.repeat(edge_y[None, :], 8, axis=0)),
-        ends_x=single(ends_x),
-        ends_y=single(ends_y),
+        pull_x=single(inverse * edge_x[:, None]),
+        pull_y=single(inverse * edge_y[None, :]),
     )
     face = dict(
-        cross=single(cross),
-        cross_t=single(cross.T),
-        cos_x=single(cos_x),
-        cos_xt=single(cos_x.T),
+        cross_e=right_const(cross[: lx // 2]),
+        cross_o=right_const(cross[lx // 2 :]),
+        cross_te=right_const(cross.T[: ly // 2]),
+        cross_to=right_const(cross.T[ly // 2 :]),
+        cos_x=right_const(cos_x),
+        cos_xt=right_const(cos_x.T),
         gap_x=single(gap_x),
         gap_y=single(gap_y.reshape(-1, lx)),
-        fourier=single(fourier),
+        fourier=right_const(fourier),
         twist=single(twist.reshape(-1, lx)),
-        gather=single(gather),
-        scatter=single(scatter),
+        gather=left_const(gather),
+        scatter=left_const(scatter),
         self_x=single(np.stack([(edge_x[:, None] ** 2 * inverse)[h].sum(0) for h in np.split(np.arange(lx), 2)])),
         self_y=single(np.stack([(edge_y**2 * inverse)[:, h].sum(1) for h in np.split(np.arange(ly), 2)])),
     )
     return main, face
 
 
-def packed(tables):
+def packed(tables, strip):
     arrays, places = [], []
-    for kind, step in ((np.dtype(np.float32), 8), (np.dtype(jnp.bfloat16), 16)):
+    for kind, step in ((np.dtype(jnp.bfloat16), 16), (np.dtype(np.float32), 8)):
         strips, start = [], 0
         for name, table in tables.items():
             if table.dtype != kind:
                 continue
-            rows, cols = -(-table.shape[0] // step) * step, -(-table.shape[1] // 128) * 128
+            rows, cols = -(-table.shape[0] // step) * step, -(-table.shape[1] // strip) * strip
             wide = np.zeros((rows, cols), kind)
             wide[: table.shape[0], : table.shape[1]] = table
-            for j in range(cols // 128):
-                strips.append(wide[:, j * 128 : (j + 1) * 128])
-                places.append((name, len(arrays), start, rows, j, cols))
+            for j in range(0, cols, strip):
+                strips.append(wide[:, j : j + strip])
+                places.append((name, len(arrays), start, *table.shape))
                 start += rows
         arrays.append(np.concatenate(strips, axis=0))
     return arrays, places
+
+
+class Table:
+    def __init__(self, ref, starts, rows, cols):
+        self.ref, self.starts, self.shape = ref, starts, (rows, cols)
+
+    def __getitem__(self, index):
+        index = (slice(None), slice(None)) if index is Ellipsis else index
+        (top, bottom, _), (left, right, _) = [part.indices(size) for part, size in zip(index, self.shape)]
+        strip = self.ref.shape[1]
+        pieces = []
+        for j, start in enumerate(self.starts):
+            low, high = max(left - j * strip, 0), min(right - j * strip, strip)
+            if low < high:
+                pieces.append(self.ref[start + top : start + bottom, low:high])
+        return pieces[0] if len(pieces) == 1 else jnp.concatenate(pieces, axis=1)
+
+
+def unpacked(refs, places):
+    starts, found = {}, {}
+    for name, which, start, rows, cols in places:
+        starts.setdefault(name, []).append(start)
+        found[name] = Table(refs[which], starts[name], rows, cols)
+    return found
 
 
 def halves(x):
@@ -234,28 +249,35 @@
         store(k, jnp.concatenate([*top, side], axis=1))
 
 
-def row_piece(ref, k, start, count):
-    return jnp.concatenate([ref[k, start + j : start + j + 1, :] for j in range(count)], axis=1)
-
-
-def transform_back(spec, group, corrs, tabs):
-    lx, ly = spec.shape[1:]
+def wide_rows(ref, start, count):
+    return jnp.concatenate([ref[:, start + j, :] for j in range(count)], axis=1)
+
+
+def flux_columns(corrs, kinds, lx, ly):
     nx, ny = lx // 128, ly // 128
-    row = lax.broadcasted_iota(jnp.int32, (8, 1), 0)
+    rows = jnp.concatenate(
+        [sum(wide_rows(corr, 2 * ny + n * nx, nx)[:kinds] for corr in corrs) for n in range(2)], axis=0
+    )
+    rows = jnp.concatenate([rows, jnp.zeros((128 - rows.shape[0], lx), F32)], axis=0)
+    return jnp.transpose(rows)
+
+
+def transform_back(spec, group, corrs, columns, tabs):
+    kinds, lx, ly = spec.shape
+    ny = ly // 128
     spectra = []
     for k in group:
-        piece = lambda start, count: sum(row_piece(corr, k, start, count) for corr in corrs)
-        a = (
-            tabs["ends_x"][...]
-            + jnp.where(row == 2, piece(2 * ny, nx), 0.0)
-            + jnp.where(row == 3, piece(2 * ny + nx, nx), 0.0)
+        piece = lambda start: jnp.broadcast_to(
+            sum(
+                jnp.concatenate([corr[k, start + j : start + j + 1, :] for j in range(ny)], axis=1)
+                for corr in corrs
+            ),
+            (lx // 2, ly),
         )
-        b = (
-            tabs["ends_y"][...]
-            + jnp.where(row == 0, piece(0, ny), 0.0)
-            + jnp.where(row == 1, piece(ny, ny), 0.0)
-        )
-        spectra.append(spec[k] + tabs["inverse"][...] * outer_sum(a, b))
+        column = lambda at: jnp.broadcast_to(columns[:, at : at + 1], (lx, ly // 2))
+        along = jnp.concatenate([piece(0), piece(ny)], axis=0)
+        across = jnp.concatenate([column(k), column(kinds + k)], axis=1)
+        spectra.append(spec[k] + (tabs["pull_x"][...] * along + tabs["pull_y"][...] * across))
     lines = times_left(tabs["inv_x"], jnp.concatenate(spectra, axis=1))
     lines = jnp.concatenate([lines[:, i * ly : (i + 1) * ly] for i in range(len(group))], axis=0)
     fields = lines_back(lines, tabs)
@@ -288,14 +310,13 @@
         pay[d, start:, :] = block
 
 
-OUT = ("fwd_ye", "fwd_yo", "fwd_x", "inverse", "edge_x", "edge_y")
-BACK = ("inv_ye", "inv_yo", "inv_x", "inverse", "ends_x", "ends_y")
-MAIN = OUT + ("inv_ye", "inv_yo", "inv_x", "ends_x", "ends_y")
-RIM = ("cross", "cross_t", "cos_xt", "self_x", "self_y")
 GROUP = 2
+PARTS = 4
 FACE = (
-    "cross",
-    "cross_t",
+    "cross_e",
+    "cross_o",
+    "cross_te",
+    "cross_to",
     "cos_x",
     "cos_xt",
     "gap_x",
@@ -317,131 +338,74 @@
             pay[d, j : j + 1, :] = line[:, j * 128 : (j + 1) * 128]
 
 
-def edge_kernel(_, state, rows_first, rows_last, cols_first, cols_last, tiles, sem):
+def edge_kernel(_, state, rows_first, rows_last, cols_first, cols_last):
     kinds, lx = cols_first.shape
-    last = state.shape[3] - 128
-    copies = [
-        pltpu.make_async_copy(state.at[0, 0], rows_first, sem.at[0]),
-        pltpu.make_async_copy(state.at[lx - 1, 0], rows_last, sem.at[1]),
-    ]
-    for k in range(kinds):
-        for n, start in enumerate((0, last)):
-            copies.append(
-                pltpu.make_async_copy(
-                    state.at[:, 0, k, pl.ds(start, 128)],
-                    tiles.at[k, :, pl.ds(n * 128, 128)],
-                    sem.at[2 + 2 * k + n],
-                )
-            )
-    for copy in copies:
-        copy.start()
-    row = lax.broadcasted_iota(jnp.int32, (8, 256), 0)
-    lane = lax.broadcasted_iota(jnp.int32, (8, 256), 1)
-    pick = jnp.where(((row == 0) & (lane == 0)) | ((row == 1) & (lane == 255)), 1.0, 0.0)
-    pick = jnp.concatenate([pick] * 3, axis=1).astype(BF16)
-    for copy in copies[2:]:
-        copy.wait()
-    for k in range(kinds):
-        cells = jnp.concatenate(thirds(tiles[k]), axis=1).astype(BF16)
-        ends = lax.dot_general(pick, cells, (((1,), (1,)), ((), ())), preferred_element_type=F32)
-        cols_first[k : k + 1, :] = ends[0:1]
-        cols_last[k : k + 1, :] = ends[1:2]
-    for copy in copies[:2]:
-        copy.wait()
-
-
-def start_kernel(parts, names, places, state, mob_hbm, *refs):
-    packs, refs = refs[:2], refs[2:]
-    count = len(names)
-    tabs = dict(zip(names, refs[:count]))
-    cells, mob, r0, spec, line_out = refs[count : count + 5]
-    st, field, lines, base, sem, tab_sem = refs[count + 5 :]
+    last = state.shape[3] - 1
+    rows_first[...] = state[0, 0]
+    rows_last[...] = state[lx - 1, 0]
+    lane = lax.broadcasted_iota(jnp.int32, (kinds, 128), 1)
+    for start in range(0, lx, 128):
+        first_cells = jnp.zeros((kinds, 128), F32)
+        last_cells = jnp.zeros((kinds, 128), F32)
+        for x in range(128):
+            first_cells = jnp.where(lane == x, state[start + x, 0, :, :128][:, :1], first_cells)
+            last_cells = jnp.where(lane == x, state[start + x, 0, :, last - 127 :][:, 127:], last_cells)
+        cols_first[:, start : start + 128] = first_cells
+        cols_last[:, start : start + 128] = last_cells
+
+
+def in_turn(stages, count):
+    for turn in range(count + len(stages) - 1):
+        for behind, stage in enumerate(stages):
+            if 0 <= turn - behind < count:
+                stage(turn - behind)
+
+
+def start_kernel(parts, tabs, state, mob_hbm, cells, mob, r0, spec, line_out, field, lines, base, mob_sem):
     lx, kinds, ly = field.shape
     size = lx // parts
-    copies = [
-        pltpu.make_async_copy(state.at[pl.ds(c * size, size), 0], st.at[pl.ds(1 + c * size, size)], sem.at[c])
-        for c in range(parts)
-    ]
-    mob_copy = pltpu.make_async_copy(mob_hbm.at[:, 0, :], mob, sem.at[parts])
+    mob_copy = pltpu.make_async_copy(mob_hbm.at[:, 0, :], mob, mob_sem.at[0])
     mob_copy.start()
-    for copy in copies:
-        copy.start()
-    loads = {name: [] for name in names}
-    for n, (name, which, start, rows, j, _) in enumerate(places):
-        loads[name].append(
-            pltpu.make_async_copy(
-                packs[which].at[pl.ds(start, rows)], tabs[name].at[:, pl.ds(j * 128, 128)], tab_sem.at[n]
-            )
-        )
-    for name in names:
-        for copy in loads[name]:
-            copy.start()
     lane = lax.broadcasted_iota(jnp.int32, (kinds, ly), 1)
 
-    def force(start):
-        for i in range(size // 8):
-            row = pl.multiple_of(start + i * 8, 8)
-            total = sum(st[pl.ds(row + 1, 8), k, :] ** 2 for k in range(kinds))
-            base[i] = -linear_coef + 2.0 * cross_coef * total
-            rates = time_step * mob[pl.ds(row, 8), :]
+    def force(part):
+        if part == 0:
+            mob_copy.wait()
+        for row in range(part * size, (part + 1) * size, 8):
+            total = sum(state[row : row + 8, 0, k, :] ** 2 for k in range(kinds))
+            base[row // 8] = -linear_coef + 2.0 * cross_coef * total
+            rates = time_step * mob[row : row + 8, :]
             for j in range(8):
-                mid = st[row + 1 + j]
+                mid = state[row + j, 0]
+                around = state[max(row + j - 1, 0), 0] + state[min(row + j + 1, lx - 1), 0]
                 left = jnp.where(lane == 0, mid, pltpu.roll(mid, 1, 1))
                 right = jnp.where(lane == ly - 1, mid, pltpu.roll(mid, ly - 1, 1))
-                lap = (st[row + j] + st[row + 2 + j]) + (left + right) - 4.0 * mid
-                react = mid * (base[i, j : j + 1, :] + (cubic_coef - 2.0 * cross_coef) * (mid * mid))
+                lap = around + (left + right) - 4.0 * mid
+                react = mid * (base[row // 8, j : j + 1, :] + (cubic_coef - 2.0 * cross_coef) * (mid * mid))
                 field[row + j] = rates[j : j + 1, :] * (gradient_coef * lap - react)
 
-    def rows_out(start):
-        rows = field[pl.ds(start, size)].reshape(size * kinds, ly)
-        lines[pl.ds(start, size)] = lines_out(rows, tabs).reshape(size, kinds, ly)
-
-    mob_copy.wait()
-    copies[0].wait()
-    copies[1].wait()
-    st[0] = st[1]
-    force(0)
-    for copy in copies[2:]:
-        copy.wait()
-    st[lx + 1] = st[lx]
-    for name in OUT:
-        for copy in loads[name]:
-            copy.wait()
-
-    @pl.loop(1, parts)
-    def _(c):
-        rows_out(pl.multiple_of((c - 1) * size, size))
-        force(pl.multiple_of(c * size, size))
-
-    rows_out(lx - size)
-
-    @pl.loop(0, lx // 8)
-    def _(i):
-        row = pl.multiple_of(i * 8, 8)
-        for k in range(kinds):
-            cells[k, pl.ds(row, 8), :] = st[pl.ds(row + 1, 8), k, :]
-            r0[k, pl.ds(row, 8), :] = field[pl.ds(row, 8), k, :]
-
+    def rows_out(part):
+        span = slice(part * size, (part + 1) * size)
+        rows = field[span].reshape(size * kinds, ly)
+        lines[span] = lines_out(rows, tabs).reshape(size, kinds, ly)
+        for row in range(part * size, (part + 1) * size, 8):
+            for k in range(kinds):
+                cells[k, row : row + 8, :] = state[row : row + 8, 0, k, :]
+                r0[k, row : row + 8, :] = field[row : row + 8, k, :]
+
+    in_turn((force, rows_out), parts)
     for k in range(0, kinds, GROUP):
         group = list(range(k, k + GROUP))
         modes_out(
             [lines[:, g, :] for g in group], group, spec, tabs, lambda g, line: store_line(line_out, [g], line)
         )
-    for name in names:
-        for copy in loads[name]:
-            if name not in OUT:
-                copy.wait()
-
-
-def rim_kernel(gx, gy, lx, ly, *refs):
-    line, lo, hi, near_left, near_right, own_left, own_right, st, mob = refs[:9]
-    names = RIM + ("fwd_ye", "fwd_yo")
-    tabs = dict(zip(names, refs[9 : 9 + len(names)]))
-    pay, corr, rows_out, cols_out = refs[9 + len(names) :]
+
+
+def rim_kernel(gx, gy, lx, ly, tabs, *refs):
+    line, lo, hi, near_left, near_right, own_left, own_right, st, mob, pay, corr, rows_out, cols_out = refs
     kinds = line.shape[0]
     nx, ny = lx // 128, ly // 128
     hx, hy = lx // 2, ly // 2
-    dot = functools.partial(jnp.dot, precision=lax.Precision.HIGHEST, preferred_element_type=F32)
 
     def column(start, lane):
         where = jnp.where(lax.broadcasted_iota(jnp.int32, (8, 128), 1) == lane, 1.0, 0.0).astype(F32)
@@ -462,22 +426,22 @@
     rows_out[...] = rows
     cols_out[...] = cols
     rows = lines_out(rows, tabs)
-    cols = dot(cols, tabs["cos_xt"][...])
+    cols = times_right(cols, tabs["cos_xt"])
     row_even, row_odd = rows[:kinds] + rows[kinds:], rows[:kinds] - rows[kinds:]
     col_even, col_odd = cols[:kinds] + cols[kinds:], cols[:kinds] - cols[kinds:]
 
     def spread(even, odd, table, width):
-        both = dot(jnp.concatenate([even, odd], axis=0), table)
+        both = times_right(jnp.concatenate([even, odd], axis=0), tabs[table])
         lane = lax.broadcasted_iota(jnp.int32, (kinds, both.shape[1]), 1)
         return jnp.where(lane < width, both[:kinds], both[kinds:])
 
     add = [
-        tabs["self_x"][0:1, :] * row_even + spread(col_even[:, :hx], col_odd[:, :hx], tabs["cross"][:hx, :], hy),
-        tabs["self_x"][1:2, :] * row_odd + spread(col_even[:, hx:], col_odd[:, hx:], tabs["cross"][hx:, :], hy),
+        tabs["self_x"][0:1, :] * row_even + spread(col_even[:, :hx], col_odd[:, :hx], "cross_e", hy),
+        tabs["self_x"][1:2, :] * row_odd + spread(col_even[:, hx:], col_odd[:, hx:], "cross_o", hy),
         tabs["self_y"][0:1, :] * col_even
-        + spread(row_even[:, :hy], row_odd[:, :hy], tabs["cross_t"][:hy, :], hx),
+        + spread(row_even[:, :hy], row_odd[:, :hy], "cross_te", hx),
         tabs["self_y"][1:2, :] * col_odd
-        + spread(row_even[:, hy:], row_odd[:, hy:], tabs["cross_t"][hy:, :], hx),
+        + spread(row_even[:, hy:], row_odd[:, hy:], "cross_to", hx),
     ]
     add = jnp.concatenate(add, axis=1)
     share = jnp.concatenate([row_even, row_odd, col_even, col_odd], axis=1)
@@ -494,15 +458,14 @@
                 pay[pl.ds(copy * kinds * gy + p, kinds, stride=gy), j, :] = value
 
 
-def middle_kernel(gx, gy, nrow, *refs):
-    corr, rim, rim_rows, rim_cols, st, mob, _, _ = refs[:8]
-    tabs = dict(zip(MAIN, refs[8 : 8 + len(MAIN)]))
-    r0, spec, field, q1, pay, acc = refs[8 + len(MAIN) :]
+def middle_kernel(gx, gy, nrow, tabs, *refs):
+    corr, rim, rim_rows, rim_cols, st, mob, _, _, r0, spec, field, q1, pay, acc = refs
     kinds, lx, ly = r0.shape
     acc[...] = jnp.zeros_like(acc)
+    columns = flux_columns((corr, rim), kinds, lx, ly)
     for k in range(0, kinds, GROUP):
         group = list(range(k, k + GROUP))
-        for g, cells in zip(group, transform_back(spec, group, (corr, rim), tabs)):
+        for g, cells in zip(group, transform_back(spec, group, (corr, rim), columns, tabs)):
             field[g] = cells
             add_rim(r0, g, rim_rows, rim_cols)
 
@@ -544,16 +507,14 @@
     store_sums(pay, nrow, [lane_sum(acc[n]) for n in range(2)])
 
 
-def last_kernel(nrow, *refs):
-    corr, st, mob, spec, r0, q1, z1 = refs[:7]
-    tabs = dict(zip(BACK, refs[7 : 7 + len(BACK)]))
-    field, sums, acc = refs[7 + len(BACK) :]
+def last_kernel(nrow, tabs, corr, st, mob, spec, r0, q1, z1, field, sums, acc):
     kinds, lx, ly = r0.shape
     acc[...] = jnp.zeros_like(acc)
     height = corr[0, nrow + 1 : nrow + 2, :] / corr[0, nrow : nrow + 1, :]
+    columns = flux_columns((corr,), kinds, lx, ly)
     for k in range(0, kinds, GROUP):
         group = list(range(k, k + GROUP))
-        for g, cells in zip(group, transform_back(spec, group, (corr,), tabs)):
+        for g, cells in zip(group, transform_back(spec, group, (corr,), columns, tabs)):
             field[g] = cells - height[:, :1] * z1[g]
 
     @pl.loop(0, lx // 8)
@@ -584,14 +545,11 @@
     store_sums(sums, 0, [lane_sum(acc[n]) for n in range(4)])
 
 
-def face_kernel(gx, gy, lx, ly, nrow, place, pay, *refs):
-    tabs = dict(zip(FACE, refs))
-    out = refs[len(FACE)]
+def face_kernel(gx, gy, lx, ly, nrow, tabs, place, pay, out):
     nx, ny = lx // 128, ly // 128
     hx, hy = lx // 2, ly // 2
     blocks = gx * gy
-    dot = functools.partial(jnp.dot, precision=lax.Precision.HIGHEST, preferred_element_type=F32)
-    piece = lambda start, count: jnp.concatenate([pay[:, start + j, :] for j in range(count)], axis=1)
+    piece = functools.partial(wide_rows, pay)
     t_even, t_odd = piece(0, ny), piece(ny, ny)
     s_even, s_odd = piece(2 * ny, nx), piece(2 * ny + nx, nx)
 
@@ -618,39 +576,40 @@
 
     def spread(minus, plus, table, width):
         count = minus.shape[0]
-        both = dot(jnp.concatenate([minus, plus], axis=0), table)
+        both = times_right(jnp.concatenate([minus, plus], axis=0), tabs[table])
         lane = lax.broadcasted_iota(jnp.int32, (count, both.shape[1]), 1)
         return jnp.where(lane < width, -both[:count], both[count:])
 
     flux = solve_x(t_even - t_odd - turn(t_even + t_odd, -gy), gy)
     minus, plus = flux - turn(flux, gy), flux + turn(flux, gy)
-    s_even = s_even + spread(minus[:, :hy], plus[:, :hy], tabs["cross_t"][:hy, :], hx)
-    s_odd = s_odd + spread(minus[:, hy:], plus[:, hy:], tabs["cross_t"][hy:, :], hx)
+    s_even = s_even + spread(minus[:, :hy], plus[:, :hy], "cross_te", hx)
+    s_odd = s_odd + spread(minus[:, hy:], plus[:, hy:], "cross_to", hx)
     jump = s_even - s_odd - group(s_even + s_odd, 1)
-    lines = dot(tabs["gather"][:, :blocks], dot(jump, tabs["cos_x"][...]))
+    lines = times_left(tabs["gather"][:, : 3 * blocks], times_right(jump, tabs["cos_x"]))
     rows = lines.shape[0] // 2
     real, imag = lines[:rows], lines[rows:]
     cosine, sine = tabs["twist"][:rows, :], tabs["twist"][rows:, :]
     turned = jnp.concatenate([real * cosine + imag * sine, imag * cosine - real * sine], axis=0)
-    both = dot(turned, tabs["fourier"][...])
+    both = times_right(turned, tabs["fourier"])
     waves = jnp.concatenate(
         [both[:rows, :lx] + both[rows:, lx:], both[rows:, :lx] - both[:rows, lx:]], axis=0
     )
     waves = circulant(lambda d: tabs["gap_y"][2 * rows * d : 2 * rows * (d + 1), :], waves, group, gy)
-    both = dot(waves, tabs["fourier"][...])
+    both = times_right(waves, tabs["fourier"])
     real = both[:rows, :lx] - both[rows:, lx:]
     imag = both[:rows, lx:] + both[rows:, :lx]
     turned = jnp.concatenate([real * cosine - imag * sine, real * sine + imag * cosine], axis=0)
-    flow = dot(dot(tabs["scatter"][:, : 2 * rows], turned), tabs["cos_xt"][...])
+    flow = times_right(times_left(tabs["scatter"][:, : 6 * rows], turned), tabs["cos_xt"])
     flow_minus, flow_plus = flow - group(flow, -1), flow + group(flow, -1)
     row = lax.broadcasted_iota(jnp.int32, (gx, blocks), 0)
     col = lax.broadcasted_iota(jnp.int32, (gx, blocks), 1)
-    pick = jnp.where(col == row * gy + place[0], 1.0, 0.0).astype(F32)
-    chosen = dot(pick, jnp.concatenate([t_even, t_odd, flow_minus, flow_plus], axis=1))
+    pick = jnp.concatenate([jnp.where(col == row * gy + place[0], 1.0, 0.0)] * 3, axis=1).astype(BF16)
+    pool = thirds(jnp.concatenate([t_even, t_odd, flow_minus, flow_plus], axis=1))
+    chosen = jnp.dot(pick, jnp.concatenate(pool, axis=0).astype(BF16), preferred_element_type=F32)
     t_even, t_odd = chosen[:, :ly], chosen[:, ly : 2 * ly]
     minus, plus = chosen[:, 2 * ly : 2 * ly + lx], chosen[:, 2 * ly + lx :]
-    t_even = t_even + spread(minus[:, :hx], plus[:, :hx], tabs["cross"][:hx, :], hy)
-    t_odd = t_odd + spread(minus[:, hx:], plus[:, hx:], tabs["cross"][hx:, :], hy)
+    t_even = t_even + spread(minus[:, :hx], plus[:, :hx], "cross_e", hy)
+    t_odd = t_odd + spread(minus[:, hx:], plus[:, hx:], "cross_o", hy)
     flux = solve_x(t_even - t_odd - turn(t_even + t_odd, -1), 1)
     line = jnp.concatenate([turn(flux, 1) - flux, flux + turn(flux, 1), -minus, plus], axis=1)
     for j in range(line.shape[1] // 128):
@@ -660,7 +619,7 @@
         out[:, n, :] = jnp.broadcast_to(total, (gx, 128))
 
 
-def finish_kernel(nrow, sums, corr, st, z1, z2, out_hbm, out, sem):
+def finish_kernel(nrow, _, sums, corr, st, z1, z2, out_hbm, out, sem):
     beta_sq = corr[0, nrow : nrow + 1, :]
     top_left = corr[0, nrow + 1 : nrow + 2, :] / beta_sq
     beta = jnp.sqrt(beta_sq)
@@ -722,10 +681,8 @@
     lx, _, kinds, ly = state.shape
     main, face = make_tables(lx, ly, gx, gy)
     tables = {**main, **face}
-    names = list(OUT) + [name for name in tables if name not in OUT]
-    packs, places = packed(tables)
-    pick = lambda some: [tables[name] for name in some]
-    rest = lambda some: [tables[name] for name in names if name not in some]
+    packs, places = packed(tables, lx)
+    packs = [jnp.asarray(pack) for pack in packs]
     nrow = (2 * lx + 2 * ly) // 128
     width = -(-(nrow + 2) // 8) * 8
     vmem = pl.BlockSpec(memory_space=pltpu.VMEM)
@@ -742,20 +699,22 @@
         count = len(inputs)
 
         def run(*refs):
-            function(*refs[:count], *refs[count + len(keep) :])
-
-        specs = [smem if x is place else vmem for x in inputs] + [vmem] * len(keep)
+            tabs, refs = unpacked(refs[:2], places), refs[2:]
+            function(tabs, *refs[:count], *refs[count + len(keep) :])
+
+        specs = [smem if x is place else hbm if x is mobility else vmem for x in inputs]
+        specs = [vmem] * 2 + specs + [vmem] * len(keep)
         return pl.pallas_call(
             run, in_specs=specs, compiler_params=grant(GRANTS[name]), name=name, **options
-        )(*inputs, *keep)
+        )(*packs, *inputs, *keep)
 
     def faces(pay, keep):
         pay = lax.all_to_all(pay, ("gx", "gy"), split_axis=0, concat_axis=0, tiled=True)
         fluxes = kernel(
             functools.partial(face_kernel, gx, gy, lx, ly, nrow),
             "faces",
-            [place, pay, *pick(FACE)],
-            keep + rest(FACE),
+            [place, pay],
+            keep,
             out_shape=array(gx, width, 128),
             out_specs=vmem,
         )
@@ -765,41 +724,34 @@
     edges = pl.pallas_call(
         edge_kernel,
         out_shape=(rows, rows, cols, cols),
-        in_specs=[smem, hbm],
+        in_specs=[smem, vmem],
         out_specs=(vmem,) * 4,
-        scratch_shapes=[pltpu.VMEM((kinds, lx, 256), F32), dma((2 + 2 * kinds,))],
         compiler_params=grant(GRANTS["edges"]),
+        cost_estimate=pl.CostEstimate(flops=2 * 10**10, bytes_accessed=6 * 10**7, transcendentals=0),
         name="edges",
     )(place, state)
     near = halo(*edges)
-    parts = 4
-    wide = {name: (count, width) for name, _, _, count, _, width in places}
-    shapes = [jax.ShapeDtypeStruct(wide[name], tables[name].dtype) for name in names]
-    outs = pl.pallas_call(
-        functools.partial(start_kernel, parts, names, places),
-        out_shape=(*shapes, whole, array(lx, ly), whole, whole, array(kinds, width, 128)),
-        in_specs=[hbm] * 4,
-        out_specs=(vmem,) * (5 + len(names)),
+
+    st, mob, r0, spec, line = kernel(
+        functools.partial(start_kernel, PARTS),
+        "start",
+        [state, mobility],
+        [],
+        out_shape=(whole, array(lx, ly), whole, whole, array(kinds, width, 128)),
+        out_specs=(vmem,) * 5,
         scratch_shapes=[
-            pltpu.VMEM((lx + 2, kinds, ly), F32),
             pltpu.VMEM((lx, kinds, ly), F32),
             pltpu.VMEM((lx, kinds, ly), F32),
-            pltpu.VMEM((lx // parts // 8, 8, ly), F32),
-            dma((parts + 1,)),
-            dma((len(places),)),
+            pltpu.VMEM((lx // 8, 8, ly), F32),
+            dma((1,)),
         ],
-        compiler_params=grant(GRANTS["start"]),
         cost_estimate=pl.CostEstimate(flops=10**10, bytes_accessed=2 * 10**7, transcendentals=0),
-        name="start",
-    )(state, mobility, *[jnp.asarray(pack) for pack in packs])
-    tables = dict(zip(names, outs))
-    st, mob, r0, spec, line = outs[len(names) :]
-    some = RIM + ("fwd_ye", "fwd_yo")
+    )
     pay, rim, rim_rows, rim_cols = kernel(
         functools.partial(rim_kernel, gx, gy, lx, ly),
         "rim",
-        [line, *near, *edges[2:], st, mob, *pick(some)],
-        [r0, spec] + rest(some),
+        [line, *near, *edges[2:], st, mob],
+        [r0, spec],
         out_shape=(payload, array(kinds, width, 128), array(2 * kinds, ly), array(2 * kinds, lx)),
         out_specs=(vmem,) * 4,
     )
@@ -807,18 +759,18 @@
     r0, spec, z1, q1, pay = kernel(
         functools.partial(middle_kernel, gx, gy, nrow),
         "middle",
-        [corr, rim, rim_rows, rim_cols, st, mob, r0, spec, *pick(MAIN)],
-        rest(MAIN),
+        [corr, rim, rim_rows, rim_cols, st, mob, r0, spec],
+        [],
         out_shape=(whole, whole, whole, whole, payload),
         out_specs=(vmem,) * 5,
         scratch_shapes=[pltpu.VMEM((2, 8, 128), F32)],
-        input_output_aliases={6: 0, 7: 1},
+        input_output_aliases={8: 0, 9: 1},
     )
     corr = faces(pay, [st, mob, r0, spec, z1, q1])
     z2, sums = kernel(
         functools.partial(last_kernel, nrow),
         "last",
-        [corr, st, mob, spec, r0, q1, z1, *pick(BACK)],
+        [corr, st, mob, spec, r0, q1, z1],
         [],
         out_shape=(whole, array(gx * gy, 8, 128)),
         out_specs=(vmem,) * 2,
@@ -832,7 +784,7 @@
         [],
         out_shape=jax.ShapeDtypeStruct(state.shape, F32),
         out_specs=hbm,
-        scratch_shapes=[pltpu.VMEM((lx, kinds, ly), F32), dma((4,))],
+        scratch_shapes=[pltpu.VMEM((lx, kinds, ly), F32), dma((8,))],
     )
 
 

time: 116 us -> 104 us (0.90)
  Pallas kernels: 48.2 us -> 38.3 us
  local copies, waits for them, and re-layouts: 4.59 us -> 2.2 us
    pallas_call x1 -> x0, Pallas kernels: 12.6 us -> none  [body(): pl.pallas_call(functools.partial(start_kernel, parts, names, places), out...]
    pallas_call x6 -> x7, Pallas kernels: 31.8 us -> 37.7 us  [kernel(): pl.pallas_call(run, in_specs=specs, compiler_params=grant(GRANTS[name]),...]
    pallas_call x1, Pallas kernels: 3.76 us -> 0.61 us  [body(): pl.pallas_call(edge_kernel, out_shape=(rows, rows, cols, cols), in_specs=...]
    unnamed x12 -> x10, local copies, waits for them, and re-layouts: 4.59 us -> 2.2 us
  transfers between devices with their start and end apart: 4 -> 4, of which waited for: 0 -> 0; matrix products, arithmetic and copies ran while one was open for 0% -> 0% of each run, Pallas kernels for 11% -> 10%
where the time goes in v3:
time: 104 us; the launch traced here: 103 us
  blocking collectives  54.8 us (53%)
  Pallas kernels  38.3 us (37%)
  starting transfers between devices  7.8 us (8%)
  local copies, waits for them, and re-layouts  2.2 us (2%)
    pallas_call x7, Pallas kernels, kernel(): pl.pallas_call(run, in_specs=specs, compiler_params=grant(GRANTS[name]),...  37.7 us
    all_to_all x2, blocking collectives, faces(): lax.all_to_all(pay, ('gx', 'gy'), split_axis=0, concat_axis=0, tiled=True)  26 us
    all_to_all x2, blocking collectives, faces(): return lax.all_to_all(fluxes, 'gx', split_axis=0, concat_axis=0, tiled=True)  18.9 us
    all_to_all x1, blocking collectives, body(): lax.all_to_all(sums, ('gx', 'gy'), split_axis=0, concat_axis=0, tiled=True)  9.93 us
    ppermute x4, starting transfers between devices, shift(): lax.ppermute(cells, axis, [(i, (i + step) % count) for i in range(count)])  7.8 us
    unnamed x10, local copies, waits for them, and re-layouts  2.2 us
  transfers between devices with their start and end apart: 4, of which 0 were waited for; matrix products, arithmetic and copies ran while one was open for 0% of the time, Pallas kernels for 10%

profile of v3, /device:TPU:0, one launch (start us, length us, event | category | flops | bytes accessed | tf_op | source)
XLA Modules:
  0.0 103.5 jit_solution(3136181084626465099)
XLA Ops:
  0.0 0.0 copy-start.2
  0.0 2.2 %copy-done.2 = f32[256,1,8,512]{3,2,1,0:T(8,128)S(1)} copy-done((f32[256,1,8,512]{3,2,1,0:T(8,128)S(1)}, f32[256,1,8,512]{3,2,1,0:T(8,128)}, u32[]{:S(2)}) %copy-start.2) | copy-done | bytes 4194328
  2.2 0.0 copy-start
  2.2 0.0 copy-start.1
  2.2 0.0 copy-start.3
  2.2 0.0 copy-start.4
  2.2 0.6 edges.1
  2.8 0.5 collective-permute-start.2
  3.3 2.0 %collective-permute-start.3 = (f32[8,256]{1,0:T(8,128)S(1)}, f32[8,256]{1,0:T(8,128)S(1)}, u32[]{:S(2)}, u32[]{:S(2)}) collective-permute-start(f32[8,256]{1,0:T(8,128)S(1)} %get-tuple-element.29.refs_7_), channel_id=1, source_target_pairs={{0,3},{1,0},{2,1},{3,2},{4,7},{5,4},{6,5},{7,6},{8,11},{9,8},{10,9... | collective-permute-start | bytes 24584 | tf_op jit(solution)/shard_map/ppermute | solution.py:670
  5.3 2.3 %collective-permute-start = (f32[8,512]{1,0:T(8,128)S(1)}, f32[8,512]{1,0:T(8,128)S(1)}, u32[]{:S(2)}, u32[]{:S(2)}) collective-permute-start(f32[8,512]{1,0:T(8,128)S(1)} %get-tuple-element.26), channel_id=1, source_target_pairs={{0,4},{4,8},{8,12},{12,16},{16,20},{20,24},{24,28},{28,0},{1,5},{5... | collective-permute-start | bytes 49160 | tf_op jit(solution)/shard_map/ppermute | solution.py:670
  7.6 3.0 %collective-permute-start.1 = (f32[8,512]{1,0:T(8,128)S(1)}, f32[8,512]{1,0:T(8,128)S(1)}, u32[]{:S(2)}, u32[]{:S(2)}) collective-permute-start(f32[8,512]{1,0:T(8,128)S(1)} %get-tuple-element.27), channel_id=1, source_target_pairs={{0,28},{4,0},{8,4},{12,8},{16,12},{20,16},{24,20},{28,24},{1,29},{... | collective-permute-start | bytes 49160 | tf_op jit(solution)/shard_map/ppermute | solution.py:670
  10.6 0.0 copy-done
  10.6 0.0 copy-done.1
  10.6 0.0 copy-done.3
  10.6 0.0 copy-done.4
  10.6 9.9 %start.1 = (f32[8,256,512]{2,1,0:T(8,128)S(1)}, f32[256,512]{1,0:T(8,128)S(1)}, f32[8,256,512]{2,1,0:T(8,128)S(1)}, f32[8,256,512]{2,1,0:T(8,128)S(1)}, f32[8,16,128]{2,1,0:T(8,128)S(1)}) custom-call(bf16[10832,256]{1,0:T(8,128)(2,1)S(1)} %copy-done, f32[2040,256]{1,0:T(8,128)S(1)} %copy-done.1, f32[256,1,8,512]{3,2,1,0:T(8,128)S(1)} %copy-done.3, ...), custom_call_target="tpu_custom_call" | custom-call | flops 10000000000 | bytes 20000000 | tf_op jit(solution)/shard_map/start/pallas_call | solution.py:707
  20.5 0.0 collective-permute-done.2.refs_5_
  20.5 0.0 collective-permute-done.3.refs_6_
  20.5 0.0 collective-permute-done.refs_3_
  20.6 0.0 collective-permute-done.1.refs_4_
  20.6 0.9 rim.1
  21.5 13.7 %all_to_all.25.refs_3_ = f32[32,16,128]{2,1,0:T(8,128)S(1)} all-to-all(f32[32,16,128]{2,1,0:T(8,128)S(1)} %get-tuple-element.34), channel_id=1, replica_groups=mesh['gx'=8,'gy'=4] {'gx','gy'}, dimensions={0} | all-to-all | bytes 524288 | tf_op jit(solution)/shard_map/all_to_all | solution.py:712
  35.2 1.8 %faces.2 = f32[8,16,128]{2,1,0:T(8,128)S(1)} custom-call(bf16[10832,256]{1,0:T(8,128)(2,1)S(1)} %copy-done, f32[2040,256]{1,0:T(8,128)S(1)} %copy-done.1, s32[1]{0:T(128)} %bitcast._.refs_2_, f32[32,16,128]{2,1,0:T(8,128)S(1)} %all_to_all.25.refs_3_, f32[8,256,512]{2,1,0:T(8,128)S(1)} %get-tuple-element.30.refs_9_.refs_4_.refs_6_.refs_3_, ...), custom_call_target="tpu_custom_call" | custom-call | tf_op jit(solution)/shard_map/faces/pallas_call | solution.py:707
  37.0 9.5 %all_to_all.26.refs_2_ = f32[8,16,128]{2,1,0:T(8,128)S(1)} all-to-all(f32[8,16,128]{2,1,0:T(8,128)S(1)} %faces.2), channel_id=1, replica_groups=mesh['gx'=8,'gy'=4] {'gx'}, dimensions={0} | all-to-all | bytes 131072 | tf_op jit(solution)/shard_map/all_to_all | solution.py:721
  46.5 12.5 %middle.1 = (f32[8,256,512]{2,1,0:T(8,128)S(1)}, f32[8,256,512]{2,1,0:T(8,128)S(1)}, f32[8,256,512]{2,1,0:T(8,128)S(1)}, f32[8,256,512]{2,1,0:T(8,128)S(1)}, f32[32,16,128]{2,1,0:T(8,128)S(1)}) custom-call(bf16[10832,256]{1,0:T(8,128)(2,1)S(1)} %copy-done, f32[2040,256]{1,0:T(8,128)S(1)} %copy-done.1, ...), custom_call_target="tpu_custom_call", output_to_operand_aliasing={{0}: (8, {}), {1}: (9, {})} | custom-call | tf_op jit(solution)/shard_map/middle/pallas_call | solution.py:707
  59.0 12.3 %all_to_all.27.refs_3_ = f32[32,16,128]{2,1,0:T(8,128)S(1)} all-to-all(f32[32,16,128]{2,1,0:T(8,128)S(1)} %get-tuple-element.38), channel_id=1, replica_groups=mesh['gx'=8,'gy'=4] {'gx','gy'}, dimensions={0} | all-to-all | bytes 524288 | tf_op jit(solution)/shard_map/all_to_all | solution.py:712
  71.3 1.8 %faces.3 = f32[8,16,128]{2,1,0:T(8,128)S(1)} custom-call(bf16[10832,256]{1,0:T(8,128)(2,1)S(1)} %copy-done, f32[2040,256]{1,0:T(8,128)S(1)} %copy-done.1, s32[1]{0:T(128)} %bitcast._.refs_2_, f32[32,16,128]{2,1,0:T(8,128)S(1)} %all_to_all.27.refs_3_, f32[8,256,512]{2,1,0:T(8,128)S(1)} %get-tuple-element.30.refs_9_.refs_4_.refs_6_.refs_3_, ...), custom_call_target="tpu_custom_call" | custom-call | tf_op jit(solution)/shard_map/faces/pallas_call | solution.py:707
  73.1 9.4 %all_to_all.28.refs_2_.refs_3_ = f32[8,16,128]{2,1,0:T(8,128)S(1)} all-to-all(f32[8,16,128]{2,1,0:T(8,128)S(1)} %faces.3), channel_id=1, replica_groups=mesh['gx'=8,'gy'=4] {'gx'}, dimensions={0} | all-to-all | bytes 131072 | tf_op jit(solution)/shard_map/all_to_all | solution.py:721
  82.5 8.1 %last.1 = (f32[8,256,512]{2,1,0:T(8,128)S(1)}, f32[32,8,128]{2,1,0:T(8,128)S(1)}) custom-call(bf16[10832,256]{1,0:T(8,128)(2,1)S(1)} %copy-done, f32[2040,256]{1,0:T(8,128)S(1)} %copy-done.1, f32[8,16,128]{2,1,0:T(8,128)S(1)} %all_to_all.28.refs_2_.refs_3_, f32[8,256,512]{2,1,0:T(8,128)S(1)} %get-tuple-element.30.refs_9_.refs_4_.refs_6_.refs_3_, ...), custom_call_target="tpu_custom_call" | custom-call | tf_op jit(solution)/shard_map/last/pallas_call | solution.py:707
  90.6 9.9 %all_to_all.29.refs_2_ = f32[32,8,128]{2,1,0:T(8,128)S(1)} all-to-all(f32[32,8,128]{2,1,0:T(8,128)S(1)} %get-tuple-element.43), channel_id=1, replica_groups=mesh['gx'=8,'gy'=4] {'gx','gy'}, dimensions={0} | all-to-all | bytes 262144 | tf_op jit(solution)/shard_map/all_to_all | solution.py:779
  100.5 2.7 %finish.1 = f32[256,1,8,512]{3,2,1,0:T(8,128)} custom-call(bf16[10832,256]{1,0:T(8,128)(2,1)S(1)} %copy-done, f32[2040,256]{1,0:T(8,128)S(1)} %copy-done.1, f32[32,8,128]{2,1,0:T(8,128)S(1)} %all_to_all.29.refs_2_, f32[8,16,128]{2,1,0:T(8,128)S(1)} %all_to_all.28.refs_2_.refs_3_, f32[8,256,512]{2,1,0:T(8,128)S(1)} %get-tuple-element.30.refs_9_.refs_4_.refs_6_.refs_3_, ...), custom_call_target="tpu_custom_call" | custom-call | tf_op jit(solution)/shard_map/finish/pallas_call | solution.py:707
Async XLA Ops:
  0.0 2.2 %copy-start.2 = (f32[256,1,8,512]{3,2,1,0:T(8,128)S(1)}, f32[256,1,8,512]{3,2,1,0:T(8,128)}, u32[]{:S(2)}) copy-start(f32[256,1,8,512]{3,2,1,0:T(8,128)} %state.1) | copy-start | bytes 12582916
  2.2 8.4 %copy-start = (bf16[10832,256]{1,0:T(8,128)(2,1)S(1)}, bf16[10832,256]{1,0:T(8,128)(2,1)}, u32[]{:S(2)}) copy-start(bf16[10832,256]{1,0:T(8,128)(2,1)} %constant.8.clone.refs_0_) | copy-start | bytes 16637956
  2.2 8.4 %copy-start.1 = (f32[2040,256]{1,0:T(8,128)S(1)}, f32[2040,256]{1,0:T(8,128)}, u32[]{:S(2)}) copy-start(f32[2040,256]{1,0:T(8,128)} %constant.9.clone.refs_1_) | copy-start | bytes 6266884
  2.2 8.4 %copy-start.3 = (f32[256,1,8,512]{3,2,1,0:T(8,128)S(1)}, f32[256,1,8,512]{3,2,1,0:T(8,128)}, u32[]{:S(2)}) copy-start(f32[256,1,8,512]{3,2,1,0:T(8,128)} %state.1) | copy-start | bytes 12582916
  2.2 8.4 %copy-start.4 = (f32[256,1,512]{2,1,0:T(1,128)S(1)}, f32[256,1,512]{2,1,0:T(1,128)}, u32[]{:S(2)}) copy-start(f32[256,1,512]{2,1,0:T(1,128)} %refs_3_.1) | copy-start | bytes 1572868
  2.8 17.7 %collective-permute-start.2 = (f32[8,256]{1,0:T(8,128)S(1)}, f32[8,256]{1,0:T(8,128)S(1)}, u32[]{:S(2)}, u32[]{:S(2)}) collective-permute-start(f32[8,256]{1,0:T(8,128)S(1)} %get-tuple-element.28.refs_8_), channel_id=1, source_target_pairs={{0,1},{1,2},{2,3},{3,0},{4,5},{5,6},{6,7},{7,4},{8,9},{9,10},{10,1... | collective-permute-start | bytes 24584 | tf_op jit(solution)/shard_map/ppermute | solution.py:670
  3.3 17.2 %collective-permute-start.3 = (f32[8,256]{1,0:T(8,128)S(1)}, f32[8,256]{1,0:T(8,128)S(1)}, u32[]{:S(2)}, u32[]{:S(2)}) collective-permute-start(f32[8,256]{1,0:T(8,128)S(1)} %get-tuple-element.29.refs_7_), channel_id=1, source_target_pairs={{0,3},{1,0},{2,1},{3,2},{4,7},{5,4},{6,5},{7,6},{8,11},{9,8},{10,9... | collective-permute-start | bytes 24584 | tf_op jit(solution)/shard_map/ppermute | solution.py:670
  5.3 15.3 %collective-permute-start = (f32[8,512]{1,0:T(8,128)S(1)}, f32[8,512]{1,0:T(8,128)S(1)}, u32[]{:S(2)}, u32[]{:S(2)}) collective-permute-start(f32[8,512]{1,0:T(8,128)S(1)} %get-tuple-element.26), channel_id=1, source_target_pairs={{0,4},{4,8},{8,12},{12,16},{16,20},{20,24},{24,28},{28,0},{1,5},{5... | collective-permute-start | bytes 49160 | tf_op jit(solution)/shard_map/ppermute | solution.py:670
  7.6 13.0 %collective-permute-start.1 = (f32[8,512]{1,0:T(8,128)S(1)}, f32[8,512]{1,0:T(8,128)S(1)}, u32[]{:S(2)}, u32[]{:S(2)}) collective-permute-start(f32[8,512]{1,0:T(8,128)S(1)} %get-tuple-element.27), channel_id=1, source_target_pairs={{0,28},{4,0},{8,4},{12,8},{16,12},{20,16},{24,20},{28,24},{1,29},{... | collective-permute-start | bytes 49160 | tf_op jit(solution)/shard_map/ppermute | solution.py:670

commit v4 on v3

--- a/solution.py
+++ b/solution.py
@@ -18,7 +18,7 @@
 
 F32 = jnp.float32
 BF16 = jnp.bfloat16
-GRANTS = dict(edges=4, start=13, rim=4, faces=4, middle=10, last=10, finish=6)
+GRANTS = dict(edges=4, start=16, rim=4, faces=4, middle=14, last=14, finish=6)
 
 
 def cosine_table(size):
@@ -100,14 +100,14 @@
         fwd_ye=right_const(cos_y[: ly // 2, : ly // 2].T),
         fwd_yo=right_const(cos_y[ly // 2 :, : ly // 2].T),
         fwd_x=left_const(cos_x),
-        inv_ye=right_const(cos_y[: ly // 2, : ly // 2]),
-        inv_yo=right_const(cos_y[ly // 2 :, : ly // 2]),
-        inv_x=left_const(cos_x.T),
-        inverse=single(inverse),
-        edge_x=single(np.repeat(edge_x[:, None], 128, axis=1)),
-        edge_y=single(np.repeat(edge_y[None, :], 8, axis=0)),
-        pull_x=single(inverse * edge_x[:, None]),
-        pull_y=single(inverse * edge_y[None, :]),
+        inv_ye=right_const((cos_y / edge_y[:, None])[: ly // 2, : ly // 2]),
+        inv_yo=right_const((cos_y / edge_y[:, None])[ly // 2 :, : ly // 2]),
+        inv_x=left_const(cos_x.T / edge_x),
+        cross=single(cross),
+        over_x=single(np.tile(1.0 / edge_x, (8, 2))),
+        over_y=single(np.tile(1.0 / edge_y, (8, 1))),
+        pull_x=single(cross * edge_x[:, None]),
+        pull_y=single(cross * edge_y[None, :]),
     )
     face = dict(
         cross_e=right_const(cross[: lx // 2]),
@@ -228,15 +228,10 @@
     lx, ly = spec.shape[1:]
     hat = times_left(tabs["fwd_x"], jnp.concatenate(lines, axis=1))
     for i, k in enumerate(group):
-        spectrum = hat[:, i * ly : (i + 1) * ly] * tabs["inverse"][...]
+        spectrum = hat[:, i * ly : (i + 1) * ly] * tabs["cross"][...]
         spec[k] = spectrum
-        weighted = spectrum * tabs["edge_x"][:, :1]
-        top = [
-            jnp.sum(weighted[: lx // 2], axis=0, keepdims=True),
-            jnp.sum(weighted[lx // 2 :], axis=0, keepdims=True),
-        ]
-        weighted = spectrum * tabs["edge_y"][:1, :]
-        cols = [weighted[:, j * 128 : (j + 1) * 128] for j in range(ly // 128)]
+        top = [jnp.sum(half, axis=0, keepdims=True) * tabs["over_y"][:1, :] for half in (spectrum[: lx // 2], spectrum[lx // 2 :])]
+        cols = [spectrum[:, j * 128 : (j + 1) * 128] for j in range(ly // 128)]
         half = len(cols) // 2
         folded = jnp.concatenate([sum(cols[1:half], cols[0]), sum(cols[half + 1 :], cols[half])], axis=0)
         high, low = halves(folded)
@@ -246,6 +241,7 @@
             (((1,), (1,)), ((), ())),
             preferred_element_type=F32,
         )[:1]
+        side = side * tabs["over_x"][:1, :]
         store(k, jnp.concatenate([*top, side], axis=1))
 
 
@@ -310,7 +306,7 @@
         pay[d, start:, :] = block
 
 
-GROUP = 2
+GROUP = 4
 PARTS = 4
 FACE = (
     "cross_e",
@@ -469,7 +465,7 @@
             field[g] = cells
             add_rim(r0, g, rim_rows, rim_cols)
 
-    @pl.loop(0, lx // 8)
+    @pl.loop(0, lx // 8, unroll=4)
     def _(i):
         row = pl.multiple_of(i * 8, 8)
         for j in range(ly // 128):
@@ -517,7 +513,7 @@
         for g, cells in zip(group, transform_back(spec, group, (corr,), columns, tabs)):
             field[g] = cells - height[:, :1] * z1[g]
 
-    @pl.loop(0, lx // 8)
+    @pl.loop(0, lx // 8, unroll=4)
     def _(i):
         row = pl.multiple_of(i * 8, 8)
         for j in range(ly // 128):

time: 104 us -> 102 us (0.981)
  Pallas kernels: 38.3 us -> 37 us
    pallas_call x7, Pallas kernels: 37.7 us -> 36.3 us  [kernel(): pl.pallas_call(run, in_specs=specs, compiler_params=grant(GRANTS[name]),...]
    unnamed x10 -> x12, local copies, waits for them, and re-layouts: 2.2 us -> 2.21 us
where the time goes in v4:
time: 102 us
  blocking collectives  54.8 us (54%)
  Pallas kernels  37 us (36%)
  starting transfers between devices  7.8 us (8%)
  local copies, waits for them, and re-layouts  2.21 us (2%)
    pallas_call x7, Pallas kernels, kernel(): pl.pallas_call(run, in_specs=specs, compiler_params=grant(GRANTS[name]),...  36.3 us
    all_to_all x2, blocking collectives, faces(): lax.all_to_all(pay, ('gx', 'gy'), split_axis=0, concat_axis=0, tiled=True)  26 us
    all_to_all x2, blocking collectives, faces(): return lax.all_to_all(fluxes, 'gx', split_axis=0, concat_axis=0, tiled=True)  18.9 us
    all_to_all x1, blocking collectives, body(): lax.all_to_all(sums, ('gx', 'gy'), split_axis=0, concat_axis=0, tiled=True)  9.93 us
    ppermute x4, starting transfers between devices, shift(): lax.ppermute(cells, axis, [(i, (i + step) % count) for i in range(count)])  7.8 us
    unnamed x12, local copies, waits for them, and re-layouts  2.21 us
  transfers between devices with their start and end apart: 4, of which 0 were waited for; matrix products, arithmetic and copies ran while one was open for 0% of the time, Pallas kernels for 10%

profile of v4, /device:TPU:0, one launch (start us, length us, event | category | flops | bytes accessed | tf_op | source)
XLA Modules:
  0.0 102.1 jit_solution(1157669220408445932)
XLA Ops:
  0.0 0.0 copy-start.3
  0.0 2.2 %copy-done.3 = f32[256,1,8,512]{3,2,1,0:T(8,128)S(1)} copy-done((f32[256,1,8,512]{3,2,1,0:T(8,128)S(1)}, f32[256,1,8,512]{3,2,1,0:T(8,128)}, u32[]{:S(2)}) %copy-start.3) | copy-done | bytes 4194328
  2.2 0.0 copy-start
  2.2 0.0 copy-start.1
  2.2 0.0 copy-start.4
  2.2 0.0 copy-start.5
  2.2 0.6 edges.1
  2.8 0.5 collective-permute-start.2
  3.3 2.0 %collective-permute-start.3 = (f32[8,256]{1,0:T(8,128)S(1)}, f32[8,256]{1,0:T(8,128)S(1)}, u32[]{:S(2)}, u32[]{:S(2)}) collective-permute-start(f32[8,256]{1,0:T(8,128)S(1)} %get-tuple-element.29.refs_7_), channel_id=1, source_target_pairs={{0,3},{1,0},{2,1},{3,2},{4,7},{5,4},{6,5},{7,6},{8,11},{9,8},{10,9... | collective-permute-start | bytes 24584 | tf_op jit(solution)/shard_map/ppermute | solution.py:666
  5.3 2.3 %collective-permute-start = (f32[8,512]{1,0:T(8,128)S(1)}, f32[8,512]{1,0:T(8,128)S(1)}, u32[]{:S(2)}, u32[]{:S(2)}) collective-permute-start(f32[8,512]{1,0:T(8,128)S(1)} %get-tuple-element.26), channel_id=1, source_target_pairs={{0,4},{4,8},{8,12},{12,16},{16,20},{20,24},{24,28},{28,0},{1,5},{5... | collective-permute-start | bytes 49160 | tf_op jit(solution)/shard_map/ppermute | solution.py:666
  7.6 3.0 %collective-permute-start.1 = (f32[8,512]{1,0:T(8,128)S(1)}, f32[8,512]{1,0:T(8,128)S(1)}, u32[]{:S(2)}, u32[]{:S(2)}) collective-permute-start(f32[8,512]{1,0:T(8,128)S(1)} %get-tuple-element.27), channel_id=1, source_target_pairs={{0,28},{4,0},{8,4},{12,8},{16,12},{20,16},{24,20},{28,24},{1,29},{... | collective-permute-start | bytes 49160 | tf_op jit(solution)/shard_map/ppermute | solution.py:666
  10.6 0.0 copy-done
  10.6 0.0 copy-done.1
  10.6 0.0 copy-done.4
  10.6 0.0 copy-done.5
  10.6 10.0 %start.1 = (f32[8,256,512]{2,1,0:T(8,128)S(1)}, f32[256,512]{1,0:T(8,128)S(1)}, f32[8,256,512]{2,1,0:T(8,128)S(1)}, f32[8,256,512]{2,1,0:T(8,128)S(1)}, f32[8,16,128]{2,1,0:T(8,128)S(1)}) custom-call(bf16[10832,256]{1,0:T(8,128)(2,1)S(1)} %copy-done, f32[1800,256]{1,0:T(8,128)S(1)} %copy-done.1, f32[256,1,8,512]{3,2,1,0:T(8,128)S(1)} %copy-done.4, ...), custom_call_target="tpu_custom_call" | custom-call | flops 10000000000 | bytes 20000000 | tf_op jit(solution)/shard_map/start/pallas_call | solution.py:703
  20.6 0.0 collective-permute-done.2.refs_5_
  20.6 0.0 collective-permute-done.3.refs_6_
  20.6 0.0 collective-permute-done.refs_3_
  20.6 0.0 collective-permute-done.1.refs_4_
  20.6 0.9 rim.1
  21.6 13.7 %all_to_all.25.refs_3_ = f32[32,16,128]{2,1,0:T(8,128)S(1)} all-to-all(f32[32,16,128]{2,1,0:T(8,128)S(1)} %get-tuple-element.34), channel_id=1, replica_groups=mesh['gx'=8,'gy'=4] {'gx','gy'}, dimensions={0} | all-to-all | bytes 524288 | tf_op jit(solution)/shard_map/all_to_all | solution.py:708
  35.3 1.8 %faces.2 = f32[8,16,128]{2,1,0:T(8,128)S(1)} custom-call(bf16[10832,256]{1,0:T(8,128)(2,1)S(1)} %copy-done, f32[1800,256]{1,0:T(8,128)S(1)} %copy-done.1, s32[1]{0:T(128)} %bitcast._.refs_2_, f32[32,16,128]{2,1,0:T(8,128)S(1)} %all_to_all.25.refs_3_, f32[8,256,512]{2,1,0:T(8,128)S(1)} %get-tuple-element.30.refs_9_.refs_4_.refs_6_.refs_3_, ...), custom_call_target="tpu_custom_call" | custom-call | tf_op jit(solution)/shard_map/faces/pallas_call | solution.py:703
  37.1 9.5 %all_to_all.26.refs_2_ = f32[8,16,128]{2,1,0:T(8,128)S(1)} all-to-all(f32[8,16,128]{2,1,0:T(8,128)S(1)} %faces.2), channel_id=1, replica_groups=mesh['gx'=8,'gy'=4] {'gx'}, dimensions={0} | all-to-all | bytes 131072 | tf_op jit(solution)/shard_map/all_to_all | solution.py:717
  46.6 11.3 %middle.1 = (f32[8,256,512]{2,1,0:T(8,128)S(1)}, f32[8,256,512]{2,1,0:T(8,128)S(1)}, f32[8,256,512]{2,1,0:T(8,128)S(1)}, f32[8,256,512]{2,1,0:T(8,128)S(1)}, f32[32,16,128]{2,1,0:T(8,128)S(1)}) custom-call(bf16[10832,256]{1,0:T(8,128)(2,1)S(1)} %copy-done, f32[1800,256]{1,0:T(8,128)S(1)} %copy-done.1, ...), custom_call_target="tpu_custom_call", output_to_operand_aliasing={{0}: (8, {}), {1}: (9, {})} | custom-call | tf_op jit(solution)/shard_map/middle/pallas_call | solution.py:703
  57.9 12.3 %all_to_all.27.refs_3_ = f32[32,16,128]{2,1,0:T(8,128)S(1)} all-to-all(f32[32,16,128]{2,1,0:T(8,128)S(1)} %get-tuple-element.38), channel_id=1, replica_groups=mesh['gx'=8,'gy'=4] {'gx','gy'}, dimensions={0} | all-to-all | bytes 524288 | tf_op jit(solution)/shard_map/all_to_all | solution.py:708
  70.2 1.8 %faces.3 = f32[8,16,128]{2,1,0:T(8,128)S(1)} custom-call(bf16[10832,256]{1,0:T(8,128)(2,1)S(1)} %copy-done, f32[1800,256]{1,0:T(8,128)S(1)} %copy-done.1, s32[1]{0:T(128)} %bitcast._.refs_2_, f32[32,16,128]{2,1,0:T(8,128)S(1)} %all_to_all.27.refs_3_, f32[8,256,512]{2,1,0:T(8,128)S(1)} %get-tuple-element.30.refs_9_.refs_4_.refs_6_.refs_3_, ...), custom_call_target="tpu_custom_call" | custom-call | tf_op jit(solution)/shard_map/faces/pallas_call | solution.py:703
  72.0 9.4 %all_to_all.28.refs_2_.refs_3_ = f32[8,16,128]{2,1,0:T(8,128)S(1)} all-to-all(f32[8,16,128]{2,1,0:T(8,128)S(1)} %faces.3), channel_id=1, replica_groups=mesh['gx'=8,'gy'=4] {'gx'}, dimensions={0} | all-to-all | bytes 131072 | tf_op jit(solution)/shard_map/all_to_all | solution.py:717
  81.4 7.8 %last.1 = (f32[8,256,512]{2,1,0:T(8,128)S(1)}, f32[32,8,128]{2,1,0:T(8,128)S(1)}) custom-call(bf16[10832,256]{1,0:T(8,128)(2,1)S(1)} %copy-done, f32[1800,256]{1,0:T(8,128)S(1)} %copy-done.1, f32[8,16,128]{2,1,0:T(8,128)S(1)} %all_to_all.28.refs_2_.refs_3_, f32[8,256,512]{2,1,0:T(8,128)S(1)} %get-tuple-element.30.refs_9_.refs_4_.refs_6_.refs_3_, ...), custom_call_target="tpu_custom_call" | custom-call | tf_op jit(solution)/shard_map/last/pallas_call | solution.py:703
  89.2 9.9 %all_to_all.29.refs_2_ = f32[32,8,128]{2,1,0:T(8,128)S(1)} all-to-all(f32[32,8,128]{2,1,0:T(8,128)S(1)} %get-tuple-element.43), channel_id=1, replica_groups=mesh['gx'=8,'gy'=4] {'gx','gy'}, dimensions={0} | all-to-all | bytes 262144 | tf_op jit(solution)/shard_map/all_to_all | solution.py:775
  99.2 0.0 copy-done.2
  99.2 2.7 %finish.1 = f32[256,1,8,512]{3,2,1,0:T(8,128)} custom-call(bf16[10832,256]{1,0:T(8,128)(2,1)S(1)} %copy-done, f32[1800,256]{1,0:T(8,128)S(1)} %copy-done.2, f32[32,8,128]{2,1,0:T(8,128)S(1)} %all_to_all.29.refs_2_, f32[8,16,128]{2,1,0:T(8,128)S(1)} %all_to_all.28.refs_2_.refs_3_, f32[8,256,512]{2,1,0:T(8,128)S(1)} %get-tuple-element.30.refs_9_.refs_4_.refs_6_.refs_3_, ...), custom_call_target="tpu_custom_call" | custom-call | tf_op jit(solution)/shard_map/finish/pallas_call | solution.py:703
  (1 shorter events, 0.0 us)
Async XLA Ops:
  0.0 2.2 %copy-start.3 = (f32[256,1,8,512]{3,2,1,0:T(8,128)S(1)}, f32[256,1,8,512]{3,2,1,0:T(8,128)}, u32[]{:S(2)}) copy-start(f32[256,1,8,512]{3,2,1,0:T(8,128)} %state.1) | copy-start | bytes 12582916
  2.2 8.4 %copy-start = (bf16[10832,256]{1,0:T(8,128)(2,1)S(1)}, bf16[10832,256]{1,0:T(8,128)(2,1)}, u32[]{:S(2)}) copy-start(bf16[10832,256]{1,0:T(8,128)(2,1)} %constant.8.clone.refs_0_) | copy-start | bytes 16637956
  2.2 8.4 %copy-start.1 = (f32[1800,256]{1,0:T(8,128)S(1)}, f32[1800,256]{1,0:T(8,128)}, u32[]{:S(2)}) copy-start(f32[1800,256]{1,0:T(8,128)} %constant.9.clone.refs_1_) | copy-start | bytes 5529604
  2.2 8.4 %copy-start.4 = (f32[256,1,8,512]{3,2,1,0:T(8,128)S(1)}, f32[256,1,8,512]{3,2,1,0:T(8,128)}, u32[]{:S(2)}) copy-start(f32[256,1,8,512]{3,2,1,0:T(8,128)} %state.1) | copy-start | bytes 12582916
  2.2 8.4 %copy-start.5 = (f32[256,1,512]{2,1,0:T(1,128)S(1)}, f32[256,1,512]{2,1,0:T(1,128)}, u32[]{:S(2)}) copy-start(f32[256,1,512]{2,1,0:T(1,128)} %refs_3_.1) | copy-start | bytes 1572868
  2.8 17.8 %collective-permute-start.2 = (f32[8,256]{1,0:T(8,128)S(1)}, f32[8,256]{1,0:T(8,128)S(1)}, u32[]{:S(2)}, u32[]{:S(2)}) collective-permute-start(f32[8,256]{1,0:T(8,128)S(1)} %get-tuple-element.28.refs_8_), channel_id=1, source_target_pairs={{0,1},{1,2},{2,3},{3,0},{4,5},{5,6},{6,7},{7,4},{8,9},{9,10},{10,1... | collective-permute-start | bytes 24584 | tf_op jit(solution)/shard_map/ppermute | solution.py:666
  3.3 17.3 %collective-permute-start.3 = (f32[8,256]{1,0:T(8,128)S(1)}, f32[8,256]{1,0:T(8,128)S(1)}, u32[]{:S(2)}, u32[]{:S(2)}) collective-permute-start(f32[8,256]{1,0:T(8,128)S(1)} %get-tuple-element.29.refs_7_), channel_id=1, source_target_pairs={{0,3},{1,0},{2,1},{3,2},{4,7},{5,4},{6,5},{7,6},{8,11},{9,8},{10,9... | collective-permute-start | bytes 24584 | tf_op jit(solution)/shard_map/ppermute | solution.py:666
  5.3 15.3 %collective-permute-start = (f32[8,512]{1,0:T(8,128)S(1)}, f32[8,512]{1,0:T(8,128)S(1)}, u32[]{:S(2)}, u32[]{:S(2)}) collective-permute-start(f32[8,512]{1,0:T(8,128)S(1)} %get-tuple-element.26), channel_id=1, source_target_pairs={{0,4},{4,8},{8,12},{12,16},{16,20},{20,24},{24,28},{28,0},{1,5},{5... | collective-permute-start | bytes 49160 | tf_op jit(solution)/shard_map/ppermute | solution.py:666
  7.6 13.1 %collective-permute-start.1 = (f32[8,512]{1,0:T(8,128)S(1)}, f32[8,512]{1,0:T(8,128)S(1)}, u32[]{:S(2)}, u32[]{:S(2)}) collective-permute-start(f32[8,512]{1,0:T(8,128)S(1)} %get-tuple-element.27), channel_id=1, source_target_pairs={{0,28},{4,0},{8,4},{12,8},{16,12},{20,16},{24,20},{28,24},{1,29},{... | collective-permute-start | bytes 49160 | tf_op jit(solution)/shard_map/ppermute | solution.py:666
  81.4 17.8 %copy-start.2 = (f32[1800,256]{1,0:T(8,128)S(1)}, f32[1800,256]{1,0:T(8,128)}, u32[]{:S(2)}) copy-start(f32[1800,256]{1,0:T(8,128)} %constant.9.clone.refs_1_) | copy-start | bytes 5529604
